TPU v7x, 512 devices: a whole 4x8x8 slice. The times are simulated.
512 devices in a mesh: dp: 64 (over y, z_lo, core), tensor: 8 (over x, z_hi).
Axes of the slice: x: 4, y: 8, z: 8 (z_hi: 2, z_lo: 4; z = z_hi * 4 + z_lo), core: 2. Of those that a mesh axis runs over, the one named last changes fastest.
Arguments:
- cache: bfloat16 [256, 1024, 576], P(None, ('dp', 'tensor')), may hold values from -6 to 6
- queries: bfloat16 [256, 3, 128, 576], P('dp', None, 'tensor'), may hold values from -36 to 36
- new_latent: bfloat16 [256, 3, 576], P('dp'), may hold values from -8 to 8
- lengths: int32 [256], replicated, may hold values from 256 to 1024, as said below
- assignment: int32 [256], replicated, may hold values from 0 to 255, each once
- value_weight: bfloat16 [128, 512, 128], P('tensor'), may hold values from -0.25 to 0.25
- output_weight: bfloat16 [16384, 7168], P('tensor', 'dp'), may hold values from -0.046875 to 0.046875
Outputs:
- layer_out: bfloat16 [256, 3, 7168], P(None, None, ('dp', 'tensor'))
Inputs may be any that keep to these rules, and one draw needn't show every extreme that they name: `lengths`: some request has exactly 1024 prefilled positions and some exactly 256. `assignment`: each request is held by exactly one slot.
All inputs are finite; a program needn't handle non-finite values.
Results may differ from a plain program's by a relative error of at most 0.015.
Values may be sent and summed in bfloat16 or wider, within the bound.
No kernel may reach another device: no remote copies, remote signals or barrier semaphores. Data moves between devices by JAX's collectives and lax.ppermute only.
A program may use at most 64 MiB of HBM per device.

v0:
```python
import jax
import jax.numpy as jnp
from jax import lax
from jax.sharding import PartitionSpec as P

score_scale = 192.0 ** (-0.5)
lowest = -1e30


def finish(scores, live, values):
    masked = jnp.where(live, scores, lowest)
    top = jnp.max(masked, axis=-1)
    raised = jnp.where(live, jnp.exp(masked - top[..., None]), 0.0)
    total = jnp.sum(raised, axis=-1)
    summed = jnp.einsum(
        "bshk,bkc->bshc", raised.astype(jnp.bfloat16), values, preferred_element_type=jnp.float32
    )
    return (top, total, summed)


def block_partial(query_heads, keys, places, limits, width):
    scores = (
        jnp.einsum("bshc,bkc->bshk", query_heads, keys, preferred_element_type=jnp.float32)
        * score_scale
    )
    live = (places[None, :] < limits[:, None])[:, None, None, :]
    return finish(scores, live, keys[:, :, :width])


def new_partial(query_heads, new_latent, width):
    step_count = new_latent.shape[1]
    scores = (
        jnp.einsum("bshc,bkc->bshk", query_heads, new_latent, preferred_element_type=jnp.float32)
        * score_scale
    )
    order = jnp.arange(step_count)
    live = (order[None, :] <= order[:, None])[None, :, None, :]
    return finish(scores, live, new_latent[:, :, :width])


def combine(first, second):
    top = jnp.maximum(first[0], second[0])
    scale_one = jnp.exp(first[0] - top)
    scale_two = jnp.exp(second[0] - top)
    total = first[1] * scale_one + second[1] * scale_two
    summed = first[2] * scale_one[..., None] + second[2] * scale_two[..., None]
    return (top, total, summed)


def on_device(cache, queries, new_latent, lengths, assignment, value_weight, output_weight):
    dp_count = lax.axis_size("dp")
    group_count = lax.axis_size("tensor")
    dp_place = lax.axis_index("dp")
    slot_count = queries.shape[0]
    step_count = queries.shape[1]
    block_rows = cache.shape[1]
    width = value_weight.shape[1]
    local_rows = dp_count * block_rows
    slot_lengths = jnp.take(lengths, assignment)
    own_limits = lax.dynamic_slice_in_dim(slot_lengths, dp_place * slot_count, slot_count)
    ordered = jnp.take(cache, assignment, axis=0)
    received = lax.all_to_all(ordered, "dp", split_axis=0, concat_axis=1, tiled=True)
    start_state = new_partial(queries, new_latent, width)
    piece = lax.all_gather(received, "tensor", axis=1, tiled=True)
    index = jnp.arange(piece.shape[1])
    member = index // local_rows
    within = index % local_rows
    places = (within // block_rows * group_count + member) * block_rows + within % block_rows
    top, total, summed = combine(
        start_state, block_partial(queries, piece, places, own_limits, width)
    )
    latent_out = (summed / total[..., None]).astype(jnp.bfloat16)
    head_out = jnp.einsum(
        "bshc,hcv->bshv", latent_out, value_weight, preferred_element_type=jnp.float32
    ).astype(jnp.bfloat16)
    flat = head_out.reshape(slot_count, step_count, -1)
    piece = lax.all_gather(flat, "dp", axis=0, tiled=True)
    rows = piece.shape[0]
    product = jnp.dot(
        piece.reshape(rows * step_count, -1), output_weight, preferred_element_type=jnp.float32
    )
    terms = product.reshape(rows, step_count, -1)
    return lax.psum_scatter(terms, "tensor", scatter_dimension=2, tiled=True).astype(jnp.bfloat16)


def solution(mesh):
    return jax.shard_map(
        on_device,
        mesh=mesh,
        in_specs=(
            P(None, ("dp", "tensor"), None),
            P("dp", None, "tensor", None),
            P("dp", None, None),
            P(),
            P(),
            P("tensor", None, None),
            P("tensor", "dp"),
        ),
        out_specs=P(None, None, ("dp", "tensor")),
        check_vma=False,
    )
```

profile of v0, /device:TPU:8, one launch (start us, length us, event | category | flops | bytes accessed | tf_op | source)
XLA Modules:
  0.0 379.1 jit_solution(14499106289486404767)
XLA Ops:
  6.5 0.0 copy-start
  6.5 0.0 all-gather.3.cloned.1.call-start
  6.5 0.8 compare_select_fusion
  7.4 2.0 gather_fusion
  9.4 0.0 copy-start.1
  9.4 0.7 broadcast_select_fusion.1
  10.1 2.4 copy.23
  12.5 2.1 gather_fusion.1
  14.6 0.0 copy-start.4
  14.6 1.2 broadcast_select_fusion
  15.8 33.2 %all_to_all.18 = bf16[256,2,576]{2,1,0:T(2,128)(2,1)S(1)} all-to-all(bf16[256,2,576]{2,1,0:T(2,128)(2,1)S(1)} %broadcast_select_fusion), channel_id=1, replica_groups=mesh['dp'=64,'tensor'=8] {'dp'}, dimensions={0} | all-to-all | bytes 1179648 | tf_op jit(solution)/shard_map/all_to_all | solution.py:62
  49.0 0.3 copy.24
  49.3 1.3 copy.25
  50.6 0.0 all-gather.3.cloned.1.call-update
  50.6 0.2 all-gather.5.cloned.1.call-start
  50.8 0.0 copy-done.1
  50.8 0.1 dynamic_slice.3
  50.9 0.0 copy-done.4
  51.0 0.4 fusion.67
  51.3 0.1 fusion.36
  51.4 0.1 broadcast_compare_fusion
  51.5 125.2 %all-gather.3.cloned.1.call-done = bf16[4,1024,576]{1,2,0:T(8,128)(2,1)} async-done(((bf16[4,128,576]{1,2,0:T(8,128)(2,1)}), bf16[4,1024,576]{1,2,0:T(8,128)(2,1)}) %all-gather.3.cloned.1.call-update) | async-done | bytes 4718608 | tf_op jit(solution)/shard_map/all_gather | solution.py:64
  176.7 0.0 copy-start.2
  176.7 3.6 fusion.66
  180.3 0.3 fusion.27
  180.6 0.0 copy-done.2
  180.6 1.4 fusion.18
  182.0 0.0 copy-start.3
  182.0 0.3 fusion.19
  182.4 0.0 copy-done
  182.4 0.5 fusion.23
  182.9 0.7 reshape.148
  183.5 0.0 all-gather.5.cloned.1.call-update
  183.5 1.3 dynamic-slice
  185.5 114.0 %all-gather.5.cloned.1.call-done = bf16[256,3,2048]{2,1,0:T(4,128)(2,1)} async-done(((bf16[4,3,2048]{2,1,0:T(4,128)(2,1)}), bf16[256,3,2048]{2,1,0:T(4,128)(2,1)}) %all-gather.5.cloned.1.call-update) | async-done | bytes 3145744 | tf_op jit(solution)/shard_map/all_gather | solution.py:77
  299.5 0.0 copy-done.3
  299.5 5.8 %fusion.3 = f32[256,3,112]{0,2,1:T(8,128)S(1)} fusion(bf16[256,3,2048]{2,1,0:T(4,128)(2,1)} %all-gather.5.cloned.1.call-done, bf16[2048,112]{0,1:T(8,128)(2,1)S(1)} %copy-done.3), kind=kOutput, calls=%fused_computation.6 | convolution fusion | flops 352321536 | bytes 3948544 | tf_op jit(solution)/shard_map/dot_general | solution.py:79
  305.3 66.3 %all-reduce.2 = bf16[256,3,112]{0,2,1:T(8,128)(2,1)S(1)} all-reduce(f32[256,3,112]{0,2,1:T(8,128)S(1)} %fusion.3), channel_id=2, replica_groups=mesh['dp'=64,'tensor'=8] {'tensor'}, use_global_device_ids=true, to_apply=%region_4.5.clone | all-reduce | flops 86016 | bytes 516096
  371.6 0.6 dynamic-slice_convert_fusion
  (6 shorter events, 0.1 us)
Async XLA Ops:
  6.5 175.8 %copy-start = (bf16[16,512,128]{2,1,0:T(8,128)(2,1)S(1)}, bf16[16,512,128]{2,1,0:T(8,128)(2,1)}, u32[]{:S(2)}) copy-start(bf16[16,512,128]{2,1,0:T(8,128)(2,1)} %param.12) | copy-start | bytes 6291460
  6.5 170.2 %all-gather.3.cloned.1.call-start = ((), (), s32[]{:S(2)}) async-start(), calls=%async_computation.1 | async-start | bytes 5308416 | tf_op jit(solution)/shard_map/all_gather | solution.py:64
  9.4 41.5 %copy-start.1 = (bf16[4,3,576]{2,0,1:T(4,128)(2,1)S(1)}, bf16[4,3,576]{2,0,1:T(4,128)(2,1)}, u32[]{:S(2)}) copy-start(bf16[4,3,576]{2,0,1:T(4,128)(2,1)} %param.9) | copy-start | bytes 41476
  14.6 36.4 %copy-start.4 = (bf16[4,3,16,576]{3,2,1,0:T(8,128)(2,1)S(1)}, bf16[4,3,16,576]{3,2,1,0:T(8,128)(2,1)}, u32[]{:S(2)}) copy-start(bf16[4,3,16,576]{3,2,1,0:T(8,128)(2,1)} %param.8) | copy-start | bytes 663556
  50.6 248.9 %all-gather.5.cloned.1.call-start = ((), (), s32[]{:S(2)}) async-start(), calls=%async_computation.2 | async-start | bytes 4259840 | tf_op jit(solution)/shard_map/all_gather | solution.py:77
  176.7 3.9 %copy-start.2 = (bf16[4,1024,576]{1,2,0:T(8,128)(2,1)S(1)}, bf16[4,1024,576]{1,2,0:T(8,128)(2,1)}, u32[]{:S(2)}) copy-start(bf16[4,1024,576]{1,2,0:T(8,128)(2,1)} %all-gather.3.cloned.1.call-done) | copy-start | bytes 14155780
  182.0 117.5 %copy-start.3 = (bf16[2048,112]{0,1:T(8,128)(2,1)S(1)}, bf16[2048,112]{0,1:T(8,128)(2,1)}, u32[]{:S(2)}) copy-start(bf16[2048,112]{0,1:T(8,128)(2,1)} %param.13) | copy-start | bytes 1376260
Sparse Core Ops, SparseCore 0:
  50.7 125.9 all-gather.2
  183.7 115.8 all-gather.4
where the time goes:
time: 379 us
  waiting for transfers between devices  239 us (63%)
  blocking collectives  99.6 us (26%)
  between operations  14.2 us (4%)
  matrix products  11.9 us (3%)
  local copies, waits for them, and re-layouts  10.7 us (3%)
    all_gather x1, waiting for transfers between devices, on_device(): piece = lax.all_gather(received, 'tensor', axis=1, tiled=True)  125 us
    all_gather x1, waiting for transfers between devices, on_device(): piece = lax.all_gather(flat, 'dp', axis=0, tiled=True)  114 us
    unnamed x1, blocking collectives  66.3 us
    all_to_all x1, blocking collectives, on_device(): lax.all_to_all(ordered, 'dp', split_axis=0, concat_axis=1, tiled=True)  33.2 us
  transfers between devices with their start and end apart: 2, of which 2 were waited for; matrix products, arithmetic and copies ran while one was open for 1% of the time, Pallas kernels for 0%

commit v1 on v0

v1 whole, which is shorter than its diff:
```python
import jax
import jax.numpy as jnp
from jax import lax
from jax.sharding import Mesh, PartitionSpec as P

score_scale = 192.0 ** (-0.5)
lowest = -1e30

DP = ("y", "za", "zb", "core")
TENSOR = ("x", "zh")
SIZES = (("y", 8), ("za", 2), ("zb", 2), ("core", 2), ("x", 4), ("zh", 2))


def swap(array, axis):
    return lax.ppermute(array, axis, [(0, 1), (1, 0)])


def in_order(own, other, axis, dim):
    first = lax.axis_index(axis) == 0
    return jnp.concatenate([jnp.where(first, own, other), jnp.where(first, other, own)], axis=dim)


def split_three(value):
    high = lax.reduce_precision(value, 8, 7)
    rest = value - high
    middle = lax.reduce_precision(rest, 8, 7)
    low = rest - middle
    return [part.astype(jnp.bfloat16) for part in (high, middle, low)]


def on_device(cache, queries, new_latent, lengths, assignment, value_weight, output_weight):
    slots, steps, heads, depth = queries.shape
    requests = cache.shape[0]
    width = value_weight.shape[1]
    vhead = value_weight.shape[2]
    x_count, zh_count = lax.axis_size("x"), lax.axis_size("zh")
    groups = x_count * zh_count
    x_place, zh_place = lax.axis_index("x"), lax.axis_index("zh")
    dp_place = lax.axis_index(DP)

    weight = output_weight.T
    weight = in_order(weight, swap(weight, "zb"), "zb", 0)
    columns = output_weight.shape[1]
    other = swap(weight, "core")
    weight = in_order(
        weight.reshape(2, 1, columns, -1), other.reshape(2, 1, columns, -1), "core", 1
    ).reshape(4 * columns, -1)

    mine = lax.all_to_all(queries, "x", split_axis=0, concat_axis=0, tiled=True)
    theirs = swap(mine, "zh")
    query = jnp.concatenate([mine, theirs], axis=0).reshape(-1, depth)

    order = (assignment[:, None] == jnp.arange(requests)[None, :]).astype(jnp.bfloat16)
    ordered = jnp.einsum(
        "jr,rpc->jpc", order, cache, preferred_element_type=jnp.float32
    ).astype(jnp.bfloat16)
    keys = lax.all_to_all(ordered, DP + ("x",), split_axis=0, concat_axis=0, tiled=True)
    block = cache.shape[1]
    keys = keys.reshape(-1, depth)
    index = jnp.arange(keys.shape[0])
    source = index // block
    places = (source // x_count * groups + source % x_count * zh_count + zh_place) * block + index % block
    slot = dp_place * slots + x_place
    limit = lengths[assignment[slot]]

    fresh = lax.dynamic_index_in_dim(new_latent, x_place, 0, keepdims=False)
    score = jnp.einsum("qc,kc->qk", query, keys, preferred_element_type=jnp.float32) * score_scale
    score = jnp.where((places < limit)[None, :], score, lowest)
    step_of = jnp.arange(query.shape[0]) // heads % steps
    live = (jnp.arange(steps)[None, :] <= step_of[:, None]) & (zh_place == 0)
    fresh_score = jnp.einsum("qc,kc->qk", query, fresh, preferred_element_type=jnp.float32) * score_scale
    fresh_score = jnp.where(live, fresh_score, lowest)
    top = jnp.maximum(jnp.max(score, axis=1), jnp.max(fresh_score, axis=1))[:, None]
    raised = jnp.exp(score - top)
    fresh_raised = jnp.exp(fresh_score - top)
    total = jnp.sum(raised, axis=1, keepdims=True) + jnp.sum(fresh_raised, axis=1, keepdims=True)
    summed = jnp.einsum(
        "qk,kc->qc", raised.astype(jnp.bfloat16), keys[:, :width], preferred_element_type=jnp.float32
    ) + jnp.einsum(
        "qk,kc->qc", fresh_raised.astype(jnp.bfloat16), fresh[:, :width], preferred_element_type=jnp.float32
    )
    partial = (summed / total).astype(jnp.bfloat16)
    marks = jnp.concatenate(split_three(top) + split_three(total), axis=1)
    marks = jnp.pad(marks, ((0, 0), (0, 128 - marks.shape[1])))
    partial = jnp.concatenate([partial, marks], axis=1)
    rows = steps * heads
    partial = partial.reshape(2, x_count, rows, width + 128)
    first = zh_place == 0
    partial = jnp.stack(
        [jnp.where(first, partial[0], partial[1]), jnp.where(first, partial[1], partial[0])], axis=1
    ).reshape(groups, rows, width + 128)

    partial = lax.all_to_all(partial, TENSOR, split_axis=0, concat_axis=0, tiled=True)
    partial = partial.reshape(x_count, zh_count, rows, -1).astype(jnp.float32)
    value, marks = partial[..., :width], partial[..., width:]
    top = marks[..., 0:1] + marks[..., 1:2] + marks[..., 2:3]
    total = marks[..., 3:4] + marks[..., 4:5] + marks[..., 5:6]
    share = total * jnp.exp(top - jnp.max(top, axis=1, keepdims=True))
    share = share / jnp.sum(share, axis=1, keepdims=True)
    latent = jnp.sum(value * share, axis=1).astype(jnp.bfloat16)
    latent = latent.reshape(slots * steps, heads, width)
    head_out = jnp.einsum(
        "rhc,hcv->rhv", latent, value_weight, preferred_element_type=jnp.float32
    ).astype(jnp.bfloat16)

    wide = ("y", "za")
    count = lax.axis_size("y") * lax.axis_size("za")
    head_out = head_out.reshape(1, slots * steps * heads // 8, vhead * 8)
    sent = jnp.broadcast_to(head_out, (count,) + head_out.shape[1:])
    piece = lax.all_to_all(sent, wide, split_axis=0, concat_axis=0, tiled=True)
    piece = piece.reshape(count * slots * steps, heads * vhead)
    product = jnp.einsum(
        "nk,mk->nm", weight, piece, preferred_element_type=jnp.float32
    ).astype(jnp.bfloat16)
    own_columns = columns // groups
    product = product.reshape(4 * groups, own_columns, -1)
    terms = lax.all_to_all(product, ("zb", "core") + TENSOR, split_axis=0, concat_axis=0, tiled=True)
    terms = terms.reshape(4, groups, own_columns, -1)
    result = jnp.sum(terms.astype(jnp.float32), axis=1).astype(jnp.bfloat16)
    result = result.reshape(4, own_columns, count, slots, steps)
    return result.transpose(2, 0, 3, 4, 1).reshape(requests, steps, own_columns)


def solution(mesh):
    names = tuple(name for name, _ in SIZES)
    fine = Mesh(mesh.devices.reshape(tuple(size for _, size in SIZES)), names)
    return jax.shard_map(
        on_device,
        mesh=fine,
        in_specs=(
            P(None, DP + TENSOR, None),
            P(DP, None, TENSOR, None),
            P(DP, None, None),
            P(),
            P(),
            P(TENSOR, None, None),
            P(TENSOR, DP),
        ),
        out_specs=P(None, None, DP + TENSOR),
        check_vma=False,
    )
```

time: 379 us -> 162 us (0.43)
  the two profiles are of different devices: /device:TPU:8 before, /device:TPU:1 now
where the time goes in v1:
time: 162 us; the launch traced here: 161 us
  waiting for transfers between devices  54.2 us (33%)
  starting transfers between devices  54 us (33%)
  local copies, waits for them, and re-layouts  17.1 us (11%)
  blocking collectives  16.8 us (10%)
  other arithmetic  9.37 us (6%)
  matrix products  6.9 us (4%)
  between operations  2.32 us (1%)
    ppermute x3, waiting for transfers between devices, swap(): return lax.ppermute(array, axis, [(0, 1), (1, 0)])  23.7 us
    all_to_all x1, waiting for transfers between devices, on_device(): piece = lax.all_to_all(sent, wide, split_axis=0, concat_axis=0, tiled=True)  20.4 us
    all_to_all x1, starting transfers between devices, on_device(): lax.all_to_all(ordered, DP + ('x',), split_axis=0, concat_axis=0, tiled=T...  18.1 us
    all_to_all x1, blocking collectives, on_device(): lax.all_to_all(product, ('zb', 'core') + TENSOR, split_axis=0, concat_axi...  16.8 us
    ppermute x3, starting transfers between devices, swap(): return lax.ppermute(array, axis, [(0, 1), (1, 0)])  13.9 us
    all_to_all x1, starting transfers between devices, on_device(): piece = lax.all_to_all(sent, wide, split_axis=0, concat_axis=0, tiled=True)  12.9 us
    all_to_all x1, waiting for transfers between devices, on_device(): lax.all_to_all(partial, TENSOR, split_axis=0, concat_axis=0, tiled=True)  8 us
    unnamed x21, local copies, waits for them, and re-layouts  7.56 us
  transfers between devices with their start and end apart: 7, of which 4 were waited for; matrix products, arithmetic and copies ran while one was open for 18% of the time, Pallas kernels for 0%

profile of v1, /device:TPU:1, one launch (start us, length us, event | category | flops | bytes accessed | tf_op | source)
XLA Modules:
  0.0 160.6 jit_solution(9768224731911262380)
XLA Ops:
  0.0 5.0 %all-to-all-start = ((bf16[4,3,16,576]{3,2,1,0:T(8,128)(2,1)}), bf16[4,3,16,576]{3,2,1,0:T(8,128)(2,1)S(1)}, u32[]{:S(2)}, u32[]{:S(2)}) async-start(bf16[4,3,16,576]{3,2,1,0:T(8,128)(2,1)} %param.8), calls=%async_computation | async-start | bytes 491520 | tf_op jit(solution)/shard_map/all_to_all | solution.py:49
  5.0 1.5 convolution_convert_fusion
  6.5 1.8 %copy.26 = bf16[256,2,576]{2,1,0:T(2,128)(2,1)} copy(bf16[256,2,576]{0,2,1:T(8,128)(2,1)S(1)} %convolution_convert_fusion) | data formatting | bytes 1179648 | tf_op jit(solution)/shard_map/convert_element_type | solution.py:56
  8.3 2.1 %all-to-all-done = bf16[4,3,16,576]{3,2,1,0:T(8,128)(2,1)S(1)} async-done(((bf16[4,3,16,576]{3,2,1,0:T(8,128)(2,1)}), bf16[4,3,16,576]{3,2,1,0:T(8,128)(2,1)S(1)}, u32[]{:S(2)}, u32[]{:S(2)}) %all-to-all-start) | async-done | bytes 221216 | tf_op jit(solution)/shard_map/all_to_all | solution.py:49
  10.4 18.1 %all-to-all-start.1 = ((bf16[256,2,576]{2,1,0:T(2,128)(2,1)}), bf16[256,2,576]{2,1,0:T(2,128)(2,1)S(1)}, u32[]{:S(2)}, u32[]{:S(2)}) async-start(bf16[256,2,576]{2,1,0:T(2,128)(2,1)} %copy.26), calls=%async_computation.1 | async-start | bytes 1310720 | tf_op jit(solution)/shard_map/all_to_all | solution.py:57
  28.5 3.3 %collective-permute-start = (bf16[112,2048]{1,0:T(8,128)(2,1)}, bf16[112,2048]{1,0:T(8,128)(2,1)}, u32[]{:S(2)}, u32[]{:S(2)}) collective-permute-start(bf16[112,2048]{1,0:T(8,128)(2,1)} %bitcast), channel_id=1, source_target_pairs={{0,16},{16,0},{1,17},{17,1},{2,18},{18,2},{3,19},{19,3},{4,20},{20... | collective-permute-start | bytes 1376264 | tf_op jit(solution)/shard_map/ppermute | solution.py:15
  31.8 0.6 dynamic_slice.10
  34.4 0.6 dynamic_slice.11
  35.0 7.9 %collective-permute-start.2 = (bf16[4,3,16,576]{3,2,1,0:T(8,128)(2,1)S(1)}, bf16[4,3,16,576]{3,2,1,0:T(8,128)(2,1)S(1)}, u32[]{:S(2)}, u32[]{:S(2)}) collective-permute-start(bf16[4,3,16,576]{3,2,1,0:T(8,128)(2,1)S(1)} %all-to-all-done), channel_id=1, source_target_pairs={{0,1},{1,0},{2,3},{3,2},{4,5},{5,4},{6,7},{7,6},{8,9},{9,8},{10,11... | collective-permute-start | bytes 663560 | tf_op jit(solution)/shard_map/ppermute | solution.py:15
  43.0 0.7 fusion.46
  43.6 23.7 %collective-permute-done.2 = bf16[4,3,16,576]{3,2,1,0:T(8,128)(2,1)S(1)} collective-permute-done((bf16[4,3,16,576]{3,2,1,0:T(8,128)(2,1)S(1)}, bf16[4,3,16,576]{3,2,1,0:T(8,128)(2,1)S(1)}, u32[]{:S(2)}, u32[]{:S(2)}) %collective-permute-start.2) | collective-permute-done | bytes 221216 | tf_op jit(solution)/shard_map/ppermute | solution.py:15
  67.4 0.3 fusion.53
  67.7 1.4 reshape.330
  69.1 1.7 %fusion.52 = (f32[384]{0:T(512)S(1)}, f32[384,512]{1,0:T(8,128)S(1)}) fusion(bf16[384,576]{1,0:T(8,128)(2,1)S(1)} %bitcast.47, bf16[512,576]{1,0:T(8,128)(2,1)} %reshape.330, pred[512]{0:T(512)(128)(4,1)S(1)} %fusion.46), kind=kOutput, calls=%fused_computation.100 | convolution fusion | flops 227081856 | bytes 1820672 | tf_op jit(solution)/shard_map/qc,kc->qk/dot_general | solution.py:67
  70.8 0.3 fusion.20
  71.2 0.3 fusion.7
  71.5 0.4 fusion.2
  72.0 0.2 copy.27
  72.3 0.8 pad_maximum_fusion.3
  73.1 4.1 %all-to-all-start.2 = ((bf16[8,48,640]{2,1,0:T(8,128)(2,1)}), bf16[8,48,640]{2,1,0:T(8,128)(2,1)}, u32[]{:S(2)}, u32[]{:S(2)}) async-start(bf16[8,48,640]{2,1,0:T(8,128)(2,1)} %bitcast.12), calls=%async_computation.2 | async-start | bytes 983040 | tf_op jit(solution)/shard_map/all_to_all | solution.py:93
  77.3 1.2 broadcast_select_fusion.3
  78.5 1.1 pad_maximum_fusion.1
  79.6 2.7 %collective-permute-start.1 = (bf16[224,2048]{1,0:T(8,128)(2,1)}, bf16[224,2048]{1,0:T(8,128)(2,1)}, u32[]{:S(2)}, u32[]{:S(2)}) collective-permute-start(bf16[224,2048]{1,0:T(8,128)(2,1)} %pad_maximum_fusion.1), channel_id=1, source_target_pairs={{0,8},{8,0},{1,9},{9,1},{2,10},{10,2},{3,11},{11,3},{4,12},{12,4},... | collective-permute-start | bytes 2752520 | tf_op jit(solution)/shard_map/ppermute | solution.py:15
  82.3 8.0 %all-to-all-done.2 = bf16[8,48,640]{2,1,0:T(8,128)(2,1)} async-done(((bf16[8,48,640]{2,1,0:T(8,128)(2,1)}), bf16[8,48,640]{2,1,0:T(8,128)(2,1)}, u32[]{:S(2)}, u32[]{:S(2)}) %all-to-all-start.2) | async-done | bytes 491552 | tf_op jit(solution)/shard_map/all_to_all | solution.py:93
  90.3 1.1 bitcast_convert_fusion
  91.4 1.4 fusion.51
  92.7 1.0 copy.46
  93.8 1.1 copy.47
  94.8 1.1 copy.48
  95.9 1.1 copy.43
  97.0 1.7 %copy.44 = f32[4,2,48,1]{2,1,0,3:T(2,128)} copy(f32[4,2,48,1]{3,2,1,0:T(8,128)} %get-tuple-element.9) | data formatting | bytes 3072
  98.6 1.6 %copy.45 = f32[4,2,48,1]{2,1,0,3:T(2,128)} copy(f32[4,2,48,1]{3,2,1,0:T(8,128)} %get-tuple-element.12) | data formatting | bytes 3072
  100.3 0.7 fusion.50
  101.0 0.1 fusion.6
  101.2 0.4 fusion.3
  101.7 1.0 broadcast_in_dim.37
  102.6 12.9 %all-to-all-start.3 = ((bf16[16,24,1024]{2,1,0:T(8,128)(2,1)}), bf16[16,24,1024]{2,1,0:T(8,128)(2,1)}, u32[]{:S(2)}, u32[]{:S(2)}) async-start(bf16[16,24,1024]{2,1,0:T(8,128)(2,1)} %broadcast_in_dim.37), calls=%async_computation.3 | async-start | bytes 1572864 | tf_op jit(solution)/shard_map/all_to_all | solution.py:110
  115.6 1.6 %broadcast_select_fusion.1 = (bf16[224,2048]{1,0:T(8,128)(2,1)S(1)}, bf16[224,2048]{1,0:T(8,128)(2,1)S(1)}) fusion(bf16[224,2048]{1,0:T(8,128)(2,1)} %collective-permute-done.1, pred[]{:T(512)S(6)} %eq.28, bf16[112,2048]{1,0:T(8,128)(2,1)S(1)} %copy-done.2, bf16[112,2048]{1,0:T(8,128)(2,1)S(1)} %get-tuple-element.15), kind=kLoop, calls=%fused_computation.16 | loop fusion | flops 2752512 | bytes 3670017 | tf_op jit(solution)/shard_map/jit(_where)/select_n | solution.py:20
  117.2 1.4 pad_maximum_fusion
  118.6 20.4 %all-to-all-done.3 = bf16[16,24,1024]{2,1,0:T(8,128)(2,1)} async-done(((bf16[16,24,1024]{2,1,0:T(8,128)(2,1)}), bf16[16,24,1024]{2,1,0:T(8,128)(2,1)}, u32[]{:S(2)}, u32[]{:S(2)}) %all-to-all-start.3) | async-done | bytes 786464 | tf_op jit(solution)/shard_map/all_to_all | solution.py:110
  139.0 1.3 reshape.332
  140.3 2.2 %convolution_convert_fusion.1 = bf16[448,192]{0,1:T(8,128)(2,1)S(1)} fusion(bf16[448,2048]{1,0:T(8,128)(2,1)} %bitcast.48, bf16[192,2048]{1,0:T(8,128)(2,1)S(1)} %reshape.332), kind=kOutput, calls=%fused_computation.7 | convolution fusion | flops 352407552 | bytes 2793472 | tf_op jit(solution)/shard_map/nk,mk->nm/dot_general | solution.py:112
  142.5 0.1 copy.38
  142.6 0.1 reshape.333
  142.7 16.8 %all_to_all.25 = bf16[32,14,192]{2,1,0:T(8,128)(2,1)S(1)} all-to-all(bf16[32,14,192]{2,1,0:T(8,128)(2,1)S(1)} %reshape.333), channel_id=1, replica_groups=mesh['y'=8,'za'=2,'zb'=2,'core'=2,'x'=4,'zh'=2] {'zb','core','x','zh'}, dimensions={0} | all-to-all | bytes 344064 | tf_op jit(solution)/shard_map/all_to_all | solution.py:117
  159.6 0.2 copy.39
  159.8 0.1 copy.40
  159.8 0.7 copy.41
  (33 shorter events, 0.5 us)
Async XLA Ops:
  0.0 101.1 %copy-start = (bf16[16,512,128]{2,1,0:T(8,128)(2,1)S(1)}, bf16[16,512,128]{2,1,0:T(8,128)(2,1)}, u32[]{:S(2)}) copy-start(bf16[16,512,128]{2,1,0:T(8,128)(2,1)} %param.12) | copy-start | bytes 6291460
  0.0 10.4 %all-to-all-start = ((bf16[4,3,16,576]{3,2,1,0:T(8,128)(2,1)}), bf16[4,3,16,576]{3,2,1,0:T(8,128)(2,1)S(1)}, u32[]{:S(2)}, u32[]{:S(2)}) async-start(bf16[4,3,16,576]{3,2,1,0:T(8,128)(2,1)} %param.8), calls=%async_computation | async-start | bytes 491520 | tf_op jit(solution)/shard_map/all_to_all | solution.py:49
  5.0 26.9 %copy-start.5 = (s32[256]{0:T(256)S(1)}, s32[256]{0:T(256)}, u32[]{:S(2)}) copy-start(s32[256]{0:T(256)} %param.11) | copy-start | bytes 3076
  5.0 28.8 %copy-start.4 = (bf16[4,3,576]{2,0,1:T(4,128)(2,1)S(1)}, bf16[4,3,576]{2,0,1:T(4,128)(2,1)}, u32[]{:S(2)}) copy-start(bf16[4,3,576]{2,0,1:T(4,128)(2,1)} %param.9) | copy-start | bytes 41476
  5.0 29.5 %copy-start.6 = (s32[256]{0:T(256)S(1)}, s32[256]{0:T(256)}, u32[]{:S(2)}) copy-start(s32[256]{0:T(256)} %param.10) | copy-start | bytes 3076
  10.4 57.3 %all-to-all-start.1 = ((bf16[256,2,576]{2,1,0:T(2,128)(2,1)}), bf16[256,2,576]{2,1,0:T(2,128)(2,1)S(1)}, u32[]{:S(2)}, u32[]{:S(2)}) async-start(bf16[256,2,576]{2,1,0:T(2,128)(2,1)} %copy.26), calls=%async_computation.1 | async-start | bytes 1310720 | tf_op jit(solution)/shard_map/all_to_all | solution.py:57
  28.5 48.7 %collective-permute-start = (bf16[112,2048]{1,0:T(8,128)(2,1)}, bf16[112,2048]{1,0:T(8,128)(2,1)}, u32[]{:S(2)}, u32[]{:S(2)}) collective-permute-start(bf16[112,2048]{1,0:T(8,128)(2,1)} %bitcast), channel_id=1, source_target_pairs={{0,16},{16,0},{1,17},{17,1},{2,18},{18,2},{3,19},{19,3},{4,20},{20... | collective-permute-start | bytes 1376264 | tf_op jit(solution)/shard_map/ppermute | solution.py:15
  35.0 32.3 %collective-permute-start.2 = (bf16[4,3,16,576]{3,2,1,0:T(8,128)(2,1)S(1)}, bf16[4,3,16,576]{3,2,1,0:T(8,128)(2,1)S(1)}, u32[]{:S(2)}, u32[]{:S(2)}) collective-permute-start(bf16[4,3,16,576]{3,2,1,0:T(8,128)(2,1)S(1)} %all-to-all-done), channel_id=1, source_target_pairs={{0,1},{1,0},{2,3},{3,2},{4,5},{5,4},{6,7},{7,6},{8,9},{9,8},{10,11... | collective-permute-start | bytes 663560 | tf_op jit(solution)/shard_map/ppermute | solution.py:15
  69.1 2.4 %copy-start.3 = (bf16[512,576]{1,0:T(8,128)(2,1)S(1)}, bf16[512,576]{1,0:T(8,128)(2,1)}, u32[]{:S(2)}) copy-start(bf16[512,576]{1,0:T(8,128)(2,1)} %reshape.330) | copy-start | bytes 1769476
  73.1 17.2 %all-to-all-start.2 = ((bf16[8,48,640]{2,1,0:T(8,128)(2,1)}), bf16[8,48,640]{2,1,0:T(8,128)(2,1)}, u32[]{:S(2)}, u32[]{:S(2)}) async-start(bf16[8,48,640]{2,1,0:T(8,128)(2,1)} %bitcast.12), calls=%async_computation.2 | async-start | bytes 983040 | tf_op jit(solution)/shard_map/all_to_all | solution.py:93
  78.5 3.8 %copy-start.1 = (bf16[112,2048]{1,0:T(8,128)(2,1)}, bf16[112,2048]{1,0:T(8,128)(2,1)S(1)}, u32[]{:S(2)}) copy-start(bf16[112,2048]{1,0:T(8,128)(2,1)S(1)} %get-tuple-element.16) | copy-start | bytes 1376260
  79.6 36.0 %collective-permute-start.1 = (bf16[224,2048]{1,0:T(8,128)(2,1)}, bf16[224,2048]{1,0:T(8,128)(2,1)}, u32[]{:S(2)}, u32[]{:S(2)}) collective-permute-start(bf16[224,2048]{1,0:T(8,128)(2,1)} %pad_maximum_fusion.1), channel_id=1, source_target_pairs={{0,8},{8,0},{1,9},{9,1},{2,10},{10,2},{3,11},{11,3},{4,12},{12,4},... | collective-permute-start | bytes 2752520 | tf_op jit(solution)/shard_map/ppermute | solution.py:15
  101.6 13.9 %copy-start.2 = (bf16[112,2048]{1,0:T(8,128)(2,1)S(1)}, bf16[112,2048]{1,0:T(8,128)(2,1)}, u32[]{:S(2)}) copy-start(bf16[112,2048]{1,0:T(8,128)(2,1)} %copy-done.1) | copy-start | bytes 1376260
  102.6 36.3 %all-to-all-start.3 = ((bf16[16,24,1024]{2,1,0:T(8,128)(2,1)}), bf16[16,24,1024]{2,1,0:T(8,128)(2,1)}, u32[]{:S(2)}, u32[]{:S(2)}) async-start(bf16[16,24,1024]{2,1,0:T(8,128)(2,1)} %broadcast_in_dim.37), calls=%async_computation.3 | async-start | bytes 1572864 | tf_op jit(solution)/shard_map/all_to_all | solution.py:110

commit v2 on v1

v2 whole, which is shorter than its diff:
```python
import functools

import jax
import jax.numpy as jnp
import numpy as np
from jax import lax
from jax.experimental import pallas as pl
from jax.experimental.pallas import tpu as pltpu
from jax.sharding import Mesh, PartitionSpec as P

score_scale = 192.0 ** (-0.5)
lowest = -1e30

DP = ("yh", "yl", "za", "zb", "core")
TENSOR = ("x", "zh")
SIZES = (("yh", 4), ("yl", 2), ("za", 2), ("zb", 2), ("core", 2), ("x", 4), ("zh", 2))
WIDE = ("yh", "za", "zb")
BLOCKS = ("yl", "core")

VMEM = pl.BlockSpec(memory_space=pltpu.VMEM)
SMEM = pl.BlockSpec(memory_space=pltpu.SMEM)


def swap(array, axis):
    return lax.ppermute(array, axis, [(0, 1), (1, 0)])


def dot(a, b):
    return jnp.dot(a, b, preferred_element_type=jnp.float32)


def dot_rows(a, b):
    return lax.dot_general(a, b, (((1,), (1,)), ((), ())), preferred_element_type=jnp.float32)


def attend(steps, heads, width, place_ref, q0, q1, q2, q3, key_ref, fresh_ref, out_ref):
    x, limit = place_ref[0], place_ref[1]
    rows = steps * heads
    query = jnp.concatenate([q[...] for q in (q0, q1, q2, q3)], axis=0)
    keys = key_ref[...]
    fresh = fresh_ref[x]
    score = dot_rows(query, keys) * score_scale
    places = lax.broadcasted_iota(jnp.int32, (1, keys.shape[0]), 1)
    score = jnp.where(places < limit, score, lowest)
    fresh_score = dot_rows(query, fresh) * score_scale
    row = lax.broadcasted_iota(jnp.int32, fresh_score.shape, 0)
    column = lax.broadcasted_iota(jnp.int32, fresh_score.shape, 1)
    live = column <= (row % rows) // heads
    fresh_score = jnp.where(live, fresh_score, lowest)
    top = jnp.maximum(
        jnp.max(score, axis=1, keepdims=True), jnp.max(fresh_score, axis=1, keepdims=True)
    )
    raised = jnp.exp(score - top)
    fresh_raised = jnp.exp(fresh_score - top)
    total = jnp.sum(raised, axis=1, keepdims=True) + jnp.sum(fresh_raised, axis=1, keepdims=True)
    summed = dot(raised.astype(jnp.bfloat16), keys[:, :width]) + dot(
        fresh_raised.astype(jnp.bfloat16), fresh[:, :width]
    )
    latent = (summed / total).astype(jnp.bfloat16)
    for shift in range(4):
        out_ref[lax.rem(x + 4 - shift, 4)] = latent[shift * rows : (shift + 1) * rows]


def map_values(count, heads, latent_ref, pick_ref, value_ref, weight_ref, out_ref):
    latent = jnp.concatenate([latent_ref[slot] for slot in range(4)], axis=0)
    picked = dot(pick_ref[...], latent).astype(jnp.bfloat16)
    lines = out_ref.shape[1]
    half = heads // 2
    vhead = value_ref.shape[2]
    for h in range(half):
        value = dot(picked[h * lines : (h + 1) * lines], value_ref[h]) + dot(
            picked[(h + half) * lines : (h + half + 1) * lines], value_ref[h + half]
        )
        value = value.astype(jnp.bfloat16)
        for copy in range(count):
            out_ref[copy, :, h * vhead : (h + 1) * vhead] = value


def project(place_ref, piece_ref, order_ref, w0, w1, w2, w3, out_ref):
    yl, core = place_ref[0], place_ref[1]
    lines = dot(order_ref[...], piece_ref[...]).astype(jnp.bfloat16)
    rows, depth = lines.shape[0] // 2, lines.shape[1]
    groups = out_ref.shape[0] // 4
    columns = out_ref.shape[1]
    weight = jnp.concatenate([w[...] for w in (w0, w1, w2, w3)], axis=0)
    product = dot_rows(weight[:, :depth], lines[:rows]) + dot_rows(weight[:, depth:], lines[rows:])
    for block in range(4):
        other_y, other_core = block // 2, block % 2
        member = (1 - yl if other_y else yl) * 2 + (1 - core if other_core else core)
        for group in range(groups):
            start = (block * groups + group) * columns
            out_ref[member * groups + group] = product[start : start + columns].astype(jnp.bfloat16)


def pick_rows(slots_steps, heads):
    n = slots_steps
    pick = np.zeros((heads * 2 * n, n * heads), np.float32)
    for h in range(heads):
        for r in range(n):
            pick[h * 2 * n + (h // (heads // 2)) * n + r, r * heads + h] = 1.0
    return jnp.asarray(pick, jnp.bfloat16)


def order_rows(count, n):
    order = np.zeros((2 * count * n, 2 * count * n), np.float32)
    for half in range(2):
        for block in range(count):
            for r in range(n):
                order[(half * count + block) * n + r, (block * 2 + half) * n + r] = 1.0
    return jnp.asarray(order, jnp.bfloat16)


def on_device(cache, queries, new_latent, lengths, assignment, value_weight, output_weight):
    slots, steps, heads, depth = queries.shape
    requests, block = cache.shape[:2]
    width, vhead = value_weight.shape[1:]
    x_place, zh_count = lax.axis_index("x"), lax.axis_size("zh")
    groups = lax.axis_size("x") * zh_count
    rows = steps * heads

    order = (jnp.repeat(assignment, zh_count)[:, None] == jnp.arange(requests)[None, :]).astype(jnp.bfloat16)
    ordered = jnp.einsum(
        "jr,rpc->jpc", order, cache, preferred_element_type=jnp.float32
    ).astype(jnp.bfloat16)
    keys = lax.all_to_all(ordered, DP + TENSOR, split_axis=0, concat_axis=0, tiled=True)

    query = []
    for shift in range(4):
        both = lax.dynamic_index_in_dim(queries, lax.rem(x_place + shift, 4), 0, keepdims=False)
        both = both.reshape(rows, depth)
        if shift:
            both = lax.ppermute(both, "x", [(j, (j + shift) % 4) for j in range(4)])
        query.append(both)

    weight, keys, *query = lax.optimization_barrier((output_weight.T, keys, *query))
    near_weight = swap(weight, "yl")
    keys = keys.reshape(-1, depth)

    slot = lax.axis_index(DP) * slots + x_place
    places = jnp.stack([x_place, lengths[assignment[slot]]]).astype(jnp.int32)
    fresh = jnp.pad(new_latent, ((0, 0), (0, 16 - steps), (0, 0)))
    latent = pl.pallas_call(
        functools.partial(attend, steps, heads, width),
        out_shape=jax.ShapeDtypeStruct((slots, rows, width), jnp.bfloat16),
        in_specs=[SMEM] + [VMEM] * 6,
        out_specs=VMEM,
        compiler_params=pltpu.CompilerParams(vmem_limit_bytes=32 * 1024 * 1024),
        name="attend",
    )(places, *query, keys, fresh)

    latent = lax.all_to_all(latent, "x", split_axis=0, concat_axis=0, tiled=True)
    count = 1
    for axis in WIDE:
        count *= lax.axis_size(axis)
    n = slots * steps
    sent = pl.pallas_call(
        functools.partial(map_values, count, heads),
        out_shape=jax.ShapeDtypeStruct((count, 2 * n, heads // 2 * vhead), jnp.bfloat16),
        in_specs=[VMEM] * 3 + [pl.BlockSpec(memory_space=pl.ANY)],
        out_specs=VMEM,
        compiler_params=pltpu.CompilerParams(vmem_limit_bytes=32 * 1024 * 1024),
        name="map_values",
    )(latent, pick_rows(n, heads), value_weight, near_weight)

    sent = sent.reshape(count * 2 * n, heads // 2 * vhead)
    piece = lax.all_to_all(sent, WIDE, split_axis=0, concat_axis=0, tiled=True)
    weights = (weight, swap(weight, "core"), near_weight, swap(near_weight, "core"))
    own_columns = output_weight.shape[1] // groups
    blocks = jnp.stack([lax.axis_index("yl"), lax.axis_index("core")]).astype(jnp.int32)
    product = pl.pallas_call(
        project,
        out_shape=jax.ShapeDtypeStruct((4 * groups, own_columns, count * n), jnp.bfloat16),
        in_specs=[SMEM] + [VMEM] * 6,
        out_specs=VMEM,
        compiler_params=pltpu.CompilerParams(vmem_limit_bytes=32 * 1024 * 1024),
        name="project",
    )(blocks, piece, order_rows(count, n), *weights)
    terms = lax.all_to_all(product, BLOCKS + TENSOR, split_axis=0, concat_axis=0, tiled=True)
    terms = terms.reshape(4, groups, own_columns, -1)
    result = jnp.sum(terms.astype(jnp.float32), axis=1).astype(jnp.bfloat16)
    yh, yl, za, zb, core = (lax.axis_size(axis) for axis in DP)
    result = result.reshape(yl, core, own_columns, yh, za, zb, slots, steps)
    return result.transpose(3, 0, 4, 5, 1, 6, 7, 2).reshape(requests, steps, own_columns)


def solution(mesh):
    names = tuple(name for name, _ in SIZES)
    fine = Mesh(mesh.devices.reshape(tuple(size for _, size in SIZES)), names)
    return jax.shard_map(
        on_device,
        mesh=fine,
        in_specs=(
            P(None, DP + TENSOR, None),
            P(DP, None, TENSOR, None),
            P(DP, None, None),
            P(),
            P(),
            P(TENSOR, None, None),
            P(TENSOR, DP),
        ),
        out_specs=P(None, None, DP + TENSOR),
        check_vma=False,
    )
```

time: 162 us -> 139 us (0.86)
  blocking collectives: 16.8 us -> 25.5 us
  other arithmetic: 9.37 us -> 0.89 us
  starting transfers between devices: 54 us -> 46.1 us
  waiting for transfers between devices: 54.2 us -> 46.6 us
  local copies, waits for them, and re-layouts: 17.1 us -> 10.5 us
  matrix products: 6.9 us -> 0.58 us
  Pallas kernels: 0 us -> 5.67 us
    ppermute x3, waiting for transfers between devices: 23.7 us -> 1.71 us  [swap(): return lax.ppermute(array, axis, [(0, 1), (1, 0)])]
    all_to_all x4 -> x2, starting transfers between devices: 40.1 us -> 27 us  [the longest x1 22.2 us: on_device(): lax.all_to_all(ordered, DP + TENSOR, split_axis=0, concat_axis=0, tiled=T...]
    all_to_all x4 -> x2, waiting for transfers between devices: 30.5 us -> 41.8 us  [the longest x1 25.1 us: on_device(): lax.all_to_all(ordered, DP + TENSOR, split_axis=0, concat_axis=0, tiled=T...]
    ppermute x0 -> x3, starting transfers between devices: none -> 10.7 us  [on_device(): both = lax.ppermute(both, 'x', [(j, (j + shift) % 4) for j in range(4)])]
    all_to_all x1 -> x2, blocking collectives: 16.8 us -> 25.5 us  [the longest x1 17.9 us: on_device(): lax.all_to_all(product, BLOCKS + TENSOR, split_axis=0, concat_axis=0, til...]
    unnamed x21, local copies, waits for them, and re-layouts: 7.56 us -> 1.1 us
    pallas_call x0 -> x3, Pallas kernels: none -> 5.67 us  [the longest x1 2.18 us: on_device(): pl.pallas_call(functools.partial(attend, steps, heads, width), out_shape=...]
    ppermute x3, starting transfers between devices: 13.9 us -> 8.37 us  [swap(): return lax.ppermute(array, axis, [(0, 1), (1, 0)])]
  transfers between devices with their start and end apart: 7 -> 8, of which waited for: 4 -> 5; matrix products, arithmetic and copies ran while one was open for 18% -> 4% of each run, Pallas kernels for 0% -> 2%
where the time goes in v2:
time: 139 us; the launch traced here: 138 us
  waiting for transfers between devices  46.6 us (34%)
  starting transfers between devices  46.1 us (33%)
  blocking collectives  25.5 us (18%)
  local copies, waits for them, and re-layouts  10.5 us (8%)
  Pallas kernels  5.67 us (4%)
  between operations  2.34 us (2%)
    all_to_all x1, waiting for transfers between devices, on_device(): lax.all_to_all(ordered, DP + TENSOR, split_axis=0, concat_axis=0, tiled=T...  25.1 us
    all_to_all x1, starting transfers between devices, on_device(): lax.all_to_all(ordered, DP + TENSOR, split_axis=0, concat_axis=0, tiled=T...  22.2 us
    all_to_all x1, blocking collectives, on_device(): lax.all_to_all(product, BLOCKS + TENSOR, split_axis=0, concat_axis=0, til...  17.9 us
    all_to_all x1, waiting for transfers between devices, on_device(): piece = lax.all_to_all(sent, WIDE, split_axis=0, concat_axis=0, tiled=True)  16.7 us
    ppermute x3, starting transfers between devices, on_device(): both = lax.ppermute(both, 'x', [(j, (j + shift) % 4) for j in range(4)])  10.7 us
    ppermute x3, starting transfers between devices, swap(): return lax.ppermute(array, axis, [(0, 1), (1, 0)])  8.37 us
    all_to_all x1, blocking collectives, on_device(): lax.all_to_all(latent, 'x', split_axis=0, concat_axis=0, tiled=True)  7.54 us
    all_to_all x1, starting transfers between devices, on_device(): piece = lax.all_to_all(sent, WIDE, split_axis=0, concat_axis=0, tiled=True)  4.85 us
  transfers between devices with their start and end apart: 8, of which 5 were waited for; matrix products, arithmetic and copies ran while one was open for 4% of the time, Pallas kernels for 2%

profile of v2, /device:TPU:1, one launch (start us, length us, event | category | flops | bytes accessed | tf_op | source)
XLA Modules:
  0.0 138.2 jit_solution(5536746838675695831)
XLA Ops:
  0.0 0.0 copy-start
  0.0 0.8 broadcast_in_dim.4
  0.8 0.1 eq.15
  1.0 0.1 copy-done
  1.1 0.6 convolution_convert_fusion
  1.7 2.8 %copy.16 = bf16[512,2,576]{2,1,0:T(2,128)(2,1)} copy(bf16[512,2,576]{0,2,1:T(8,128)(2,1)S(1)} %convolution_convert_fusion) | data formatting | bytes 2359296 | tf_op jit(solution)/shard_map/convert_element_type | solution.py:124
  4.5 0.0 copy-start.6
  4.5 0.0 copy-start.9
  4.5 22.2 %all-to-all-start = ((bf16[512,2,576]{2,1,0:T(2,128)(2,1)}), bf16[512,2,576]{2,1,0:T(2,128)(2,1)S(1)}, u32[]{:S(2)}, u32[]{:S(2)}) async-start(bf16[512,2,576]{2,1,0:T(2,128)(2,1)} %copy.16), calls=%async_computation | async-start | bytes 2621440 | tf_op jit(solution)/shard_map/all_to_all | solution.py:125
  26.7 0.0 copy-done.6
  26.8 3.3 %collective-permute-start = (bf16[48,576]{1,0:T(8,128)(2,1)S(1)}, bf16[48,576]{1,0:T(8,128)(2,1)S(1)}, u32[]{:S(2)}, u32[]{:S(2)}) collective-permute-start(bf16[48,576]{1,0:T(8,128)(2,1)S(1)} %bitcast.29), channel_id=1, source_target_pairs={{0,2},{2,4},{4,6},{6,0},{1,3},{3,5},{5,7},{7,1},{8,10},{10,12},{12... | collective-permute-start | bytes 165896 | tf_op jit(solution)/shard_map/ppermute | solution.py:132
  30.1 4.3 %collective-permute-start.1 = (bf16[48,576]{1,0:T(8,128)(2,1)S(1)}, bf16[48,576]{1,0:T(8,128)(2,1)S(1)}, u32[]{:S(2)}, u32[]{:S(2)}) collective-permute-start(bf16[48,576]{1,0:T(8,128)(2,1)S(1)} %bitcast.28), channel_id=1, source_target_pairs={{0,4},{2,6},{4,0},{6,2},{1,5},{3,7},{5,1},{7,3},{8,12},{10,14},{12... | collective-permute-start | bytes 165896 | tf_op jit(solution)/shard_map/ppermute | solution.py:132
  34.4 3.1 %collective-permute-start.2 = (bf16[48,576]{1,0:T(8,128)(2,1)S(1)}, bf16[48,576]{1,0:T(8,128)(2,1)S(1)}, u32[]{:S(2)}, u32[]{:S(2)}) collective-permute-start(bf16[48,576]{1,0:T(8,128)(2,1)S(1)} %bitcast.27), channel_id=1, source_target_pairs={{0,6},{2,0},{4,2},{6,4},{1,7},{3,1},{5,3},{7,5},{8,14},{10,8},{12,... | collective-permute-start | bytes 165896 | tf_op jit(solution)/shard_map/ppermute | solution.py:132
  37.5 0.0 collective-permute-done.q1
  37.5 0.2 collective-permute-done.1.q2
  37.7 2.9 %collective-permute-done.2.q3 = bf16[48,576]{1,0:T(8,128)(2,1)S(1)} collective-permute-done((bf16[48,576]{1,0:T(8,128)(2,1)S(1)}, bf16[48,576]{1,0:T(8,128)(2,1)S(1)}, u32[]{:S(2)}, u32[]{:S(2)}) %collective-permute-start.2) | collective-permute-done | bytes 55328 | tf_op jit(solution)/shard_map/ppermute | solution.py:132
  40.6 25.1 %all-to-all-done = bf16[512,2,576]{2,1,0:T(2,128)(2,1)S(1)} async-done(((bf16[512,2,576]{2,1,0:T(2,128)(2,1)}), bf16[512,2,576]{2,1,0:T(2,128)(2,1)S(1)}, u32[]{:S(2)}, u32[]{:S(2)}) %all-to-all-start) | async-done | bytes 1179680 | tf_op jit(solution)/shard_map/all_to_all | solution.py:125
  65.7 0.0 copy-done.2
  65.7 2.5 %collective-permute-start.3 = (bf16[112,2048]{1,0:T(8,128)(2,1)S(1)}, bf16[112,2048]{1,0:T(8,128)(2,1)S(1)}, u32[]{:S(2)}, u32[]{:S(2)}) collective-permute-start(bf16[112,2048]{1,0:T(8,128)(2,1)S(1)} %bitcast.21), channel_id=1, source_target_pairs={{0,64},{64,0},{1,65},{65,1},{2,66},{66,2},{3,67},{67,3},{4,68},{68... | collective-permute-start | bytes 1376264 | tf_op jit(solution)/shard_map/ppermute | solution.py:25
  68.3 0.0 copy-done.8
  68.3 0.7 dynamic_slice.19
  70.4 0.0 copy-done.7
  71.1 0.0 copy-done.5
  71.1 0.0 copy-done.9
  71.1 0.7 dynamic_slice.20
  71.8 0.8 pad_add_fusion.1.place_ref
  72.6 3.2 %reshape.37.key_ref = bf16[1024,576]{1,0:T(8,128)(2,1)S(1)} reshape(bf16[512,2,576]{2,1,0:T(2,128)(2,1)} %copy-done.5) | data formatting | bytes 2359296 | tf_op jit(solution)/shard_map/reshape | solution.py:137
  75.8 0.0 copy-start.1
  75.8 2.2 %attend.1 = bf16[4,48,512]{2,1,0:T(8,128)(2,1)S(1)} custom-call(s32[2]{0:T(128)S(1)} %pad_add_fusion.1.place_ref, bf16[48,576]{1,0:T(8,128)(2,1)S(1)} %bitcast.24, bf16[48,576]{1,0:T(8,128)(2,1)S(1)} %collective-permute-done.q1, bf16[48,576]{1,0:T(8,128)(2,1)S(1)} %collective-permute-done.1.q2, bf16[48,576]{1,0:T(8,128)(2,1)S(1)} %collective-permute-done.2.q3, ...), custom_call_target="tpu_custom_call" | custom-call | tf_op jit(solution)/shard_map/attend/pallas_call | solution.py:142
  78.0 7.5 %all_to_all.23.latent_ref = bf16[4,48,512]{2,1,0:T(8,128)(2,1)S(1)} all-to-all(bf16[4,48,512]{2,1,0:T(8,128)(2,1)S(1)} %attend.1), channel_id=1, replica_groups=mesh['yh'=4,'yl'=2,'za'=2,'zb'=2,'core'=2,'x'=4,'zh'=2] {'x'}, dimensions={0} | all-to-all | bytes 393216 | tf_op jit(solution)/shard_map/all_to_all | solution.py:151
  85.5 0.0 collective-permute-done.3.weight_ref.w2
  85.6 0.0 copy-done.4
  85.6 0.0 copy-done.1
  85.6 1.6 %map_values.1 = bf16[16,24,1024]{2,1,0:T(8,128)(2,1)} custom-call(bf16[4,48,512]{2,1,0:T(8,128)(2,1)S(1)} %all_to_all.23.latent_ref, bf16[384,192]{1,0:T(8,128)(2,1)S(1)} %copy-done.4, bf16[16,512,128]{2,1,0:T(8,128)(2,1)S(1)} %copy-done.1, bf16[112,2048]{1,0:T(8,128)(2,1)S(1)} %collective-permute-done.3.weight_ref.w2), custom_call_target="tpu_custom_call" | custom-call | tf_op jit(solution)/shard_map/map_values/pallas_call | solution.py:156
  87.1 4.9 %all-to-all-start.2 = ((bf16[16,24,1024]{2,1,0:T(8,128)(2,1)}), bf16[16,24,1024]{2,1,0:T(8,128)(2,1)S(1)}, u32[]{:S(2)}, u32[]{:S(2)}) async-start(bf16[16,24,1024]{2,1,0:T(8,128)(2,1)} %map_values.1), calls=%async_computation.2 | async-start | bytes 1572864 | tf_op jit(solution)/shard_map/all_to_all | solution.py:166
  92.0 3.9 %collective-permute-start.4 = (bf16[112,2048]{1,0:T(8,128)(2,1)S(1)}, bf16[112,2048]{1,0:T(8,128)(2,1)S(1)}, u32[]{:S(2)}, u32[]{:S(2)}) collective-permute-start(bf16[112,2048]{1,0:T(8,128)(2,1)S(1)} %bitcast.22), channel_id=1, source_target_pairs={{0,8},{8,0},{1,9},{9,1},{2,10},{10,2},{3,11},{11,3},{4,12},{12,4},... | collective-permute-start | bytes 1376264 | tf_op jit(solution)/shard_map/ppermute | solution.py:25
  95.9 1.9 %collective-permute-start.5 = (bf16[112,2048]{1,0:T(8,128)(2,1)S(1)}, bf16[112,2048]{1,0:T(8,128)(2,1)S(1)}, u32[]{:S(2)}, u32[]{:S(2)}) collective-permute-start(bf16[112,2048]{1,0:T(8,128)(2,1)S(1)} %collective-permute-done.3.weight_ref.w2), channel_id=1, source_target_pairs={{0,8},{8,0},{1,9},{9,1},{2,10},{10,2},{3,11},{11,3},{4,12},{12,4},... | collective-permute-start | bytes 1376264 | tf_op jit(solution)/shard_map/ppermute | solution.py:25
  97.8 0.1 pad_add_fusion.place_ref
  97.9 0.0 collective-permute-done.4.w1
  97.9 1.7 %collective-permute-done.5.w3 = bf16[112,2048]{1,0:T(8,128)(2,1)S(1)} collective-permute-done((bf16[112,2048]{1,0:T(8,128)(2,1)S(1)}, bf16[112,2048]{1,0:T(8,128)(2,1)S(1)}, u32[]{:S(2)}, u32[]{:S(2)}) %collective-permute-start.5) | collective-permute-done | bytes 458784 | tf_op jit(solution)/shard_map/ppermute | solution.py:25
  99.6 16.7 %all-to-all-done.2 = bf16[16,24,1024]{2,1,0:T(8,128)(2,1)S(1)} async-done(((bf16[16,24,1024]{2,1,0:T(8,128)(2,1)}), bf16[16,24,1024]{2,1,0:T(8,128)(2,1)S(1)}, u32[]{:S(2)}, u32[]{:S(2)}) %all-to-all-start.2) | async-done | bytes 786464 | tf_op jit(solution)/shard_map/all_to_all | solution.py:166
  116.3 1.0 copy-done.3
  117.3 1.9 %project.1 = bf16[32,14,192]{2,1,0:T(8,128)(2,1)S(1)} custom-call(s32[2]{0:T(128)S(1)} %pad_add_fusion.place_ref, bf16[384,1024]{1,0:T(8,128)(2,1)S(1)} %bitcast.20, bf16[384,384]{1,0:T(8,128)(2,1)S(1)} %copy-done.3, bf16[112,2048]{1,0:T(8,128)(2,1)S(1)} %bitcast.23, bf16[112,2048]{1,0:T(8,128)(2,1)S(1)} %collective-permute-done.4.w1, ...), custom_call_target="tpu_custom_call" | custom-call | tf_op jit(solution)/shard_map/project/pallas_call | solution.py:170
  119.2 17.9 %all_to_all.24 = bf16[32,14,192]{2,1,0:T(8,128)(2,1)S(1)} all-to-all(bf16[32,14,192]{2,1,0:T(8,128)(2,1)S(1)} %project.1), channel_id=1, replica_groups=mesh['yh'=4,'yl'=2,'za'=2,'zb'=2,'core'=2,'x'=4,'zh'=2] {'yl','core','x'..., dimensions={0} | all-to-all | bytes 344064 | tf_op jit(solution)/shard_map/all_to_all | solution.py:178
  137.1 0.1 bitcast_reduce_fusion
  137.2 0.2 copy.18
  137.4 0.1 copy.19
  137.5 0.7 copy.20
  (9 shorter events, 0.1 us)
Async XLA Ops:
  0.0 1.1 copy-start
  4.5 22.2 %copy-start.6 = (bf16[4,3,16,576]{3,2,1,0:T(8,128)(2,1)S(1)}, bf16[4,3,16,576]{3,2,1,0:T(8,128)(2,1)}, u32[]{:S(2)}) copy-start(bf16[4,3,16,576]{3,2,1,0:T(8,128)(2,1)} %param.10) | copy-start | bytes 663556
  4.5 61.2 %copy-start.2 = (bf16[2048,112]{0,1:T(8,128)(2,1)S(1)}, bf16[2048,112]{0,1:T(8,128)(2,1)}, u32[]{:S(2)}) copy-start(bf16[2048,112]{0,1:T(8,128)(2,1)} %param.15) | copy-start | bytes 1376260
  4.5 63.8 %copy-start.8 = (s32[256]{0:T(256)S(1)}, s32[256]{0:T(256)}, u32[]{:S(2)}) copy-start(s32[256]{0:T(256)} %param.13) | copy-start | bytes 3076
  4.5 65.9 %copy-start.7 = (bf16[4,3,576]{2,0,1:T(4,128)(2,1)S(1)}, bf16[4,3,576]{2,0,1:T(4,128)(2,1)}, u32[]{:S(2)}) copy-start(bf16[4,3,576]{2,0,1:T(4,128)(2,1)} %param.11) | copy-start | bytes 41476
  4.5 66.6 %copy-start.9 = (s32[256]{0:T(256)S(1)}, s32[256]{0:T(256)}, u32[]{:S(2)}) copy-start(s32[256]{0:T(256)} %param.12) | copy-start | bytes 3076
  4.5 61.2 %all-to-all-start = ((bf16[512,2,576]{2,1,0:T(2,128)(2,1)}), bf16[512,2,576]{2,1,0:T(2,128)(2,1)S(1)}, u32[]{:S(2)}, u32[]{:S(2)}) async-start(bf16[512,2,576]{2,1,0:T(2,128)(2,1)} %copy.16), calls=%async_computation | async-start | bytes 2621440 | tf_op jit(solution)/shard_map/all_to_all | solution.py:125
  26.8 10.7 %collective-permute-start = (bf16[48,576]{1,0:T(8,128)(2,1)S(1)}, bf16[48,576]{1,0:T(8,128)(2,1)S(1)}, u32[]{:S(2)}, u32[]{:S(2)}) collective-permute-start(bf16[48,576]{1,0:T(8,128)(2,1)S(1)} %bitcast.29), channel_id=1, source_target_pairs={{0,2},{2,4},{4,6},{6,0},{1,3},{3,5},{5,7},{7,1},{8,10},{10,12},{12... | collective-permute-start | bytes 165896 | tf_op jit(solution)/shard_map/ppermute | solution.py:132
  30.1 7.6 %collective-permute-start.1 = (bf16[48,576]{1,0:T(8,128)(2,1)S(1)}, bf16[48,576]{1,0:T(8,128)(2,1)S(1)}, u32[]{:S(2)}, u32[]{:S(2)}) collective-permute-start(bf16[48,576]{1,0:T(8,128)(2,1)S(1)} %bitcast.28), channel_id=1, source_target_pairs={{0,4},{2,6},{4,0},{6,2},{1,5},{3,7},{5,1},{7,3},{8,12},{10,14},{12... | collective-permute-start | bytes 165896 | tf_op jit(solution)/shard_map/ppermute | solution.py:132
  34.4 6.2 %collective-permute-start.2 = (bf16[48,576]{1,0:T(8,128)(2,1)S(1)}, bf16[48,576]{1,0:T(8,128)(2,1)S(1)}, u32[]{:S(2)}, u32[]{:S(2)}) collective-permute-start(bf16[48,576]{1,0:T(8,128)(2,1)S(1)} %bitcast.27), channel_id=1, source_target_pairs={{0,6},{2,0},{4,2},{6,4},{1,7},{3,1},{5,3},{7,5},{8,14},{10,8},{12,... | collective-permute-start | bytes 165896 | tf_op jit(solution)/shard_map/ppermute | solution.py:132
  65.7 5.4 %copy-start.5 = (bf16[512,2,576]{2,1,0:T(2,128)(2,1)}, bf16[512,2,576]{2,1,0:T(2,128)(2,1)S(1)}, u32[]{:S(2)}) copy-start(bf16[512,2,576]{2,1,0:T(2,128)(2,1)S(1)} %all-to-all-done) | copy-start | bytes 3538948
  65.7 19.8 %collective-permute-start.3 = (bf16[112,2048]{1,0:T(8,128)(2,1)S(1)}, bf16[112,2048]{1,0:T(8,128)(2,1)S(1)}, u32[]{:S(2)}, u32[]{:S(2)}) collective-permute-start(bf16[112,2048]{1,0:T(8,128)(2,1)S(1)} %bitcast.21), channel_id=1, source_target_pairs={{0,64},{64,0},{1,65},{65,1},{2,66},{66,2},{3,67},{67,3},{4,68},{68... | collective-permute-start | bytes 1376264 | tf_op jit(solution)/shard_map/ppermute | solution.py:25
  72.6 13.0 %copy-start.4 = (bf16[384,192]{1,0:T(8,128)(2,1)S(1)}, bf16[384,192]{1,0:T(8,128)(2,1)}, u32[]{:S(2)}) copy-start(bf16[384,192]{1,0:T(8,128)(2,1)} %constant.67.clone.pick_ref) | copy-start | bytes 442372
  75.8 9.8 %copy-start.1 = (bf16[16,512,128]{2,1,0:T(8,128)(2,1)S(1)}, bf16[16,512,128]{2,1,0:T(8,128)(2,1)}, u32[]{:S(2)}) copy-start(bf16[16,512,128]{2,1,0:T(8,128)(2,1)} %value_ref.1) | copy-start | bytes 6291460
  87.1 29.2 %all-to-all-start.2 = ((bf16[16,24,1024]{2,1,0:T(8,128)(2,1)}), bf16[16,24,1024]{2,1,0:T(8,128)(2,1)S(1)}, u32[]{:S(2)}, u32[]{:S(2)}) async-start(bf16[16,24,1024]{2,1,0:T(8,128)(2,1)} %map_values.1), calls=%async_computation.2 | async-start | bytes 1572864 | tf_op jit(solution)/shard_map/all_to_all | solution.py:166
  92.0 5.9 %collective-permute-start.4 = (bf16[112,2048]{1,0:T(8,128)(2,1)S(1)}, bf16[112,2048]{1,0:T(8,128)(2,1)S(1)}, u32[]{:S(2)}, u32[]{:S(2)}) collective-permute-start(bf16[112,2048]{1,0:T(8,128)(2,1)S(1)} %bitcast.22), channel_id=1, source_target_pairs={{0,8},{8,0},{1,9},{9,1},{2,10},{10,2},{3,11},{11,3},{4,12},{12,4},... | collective-permute-start | bytes 1376264 | tf_op jit(solution)/shard_map/ppermute | solution.py:25
  95.9 3.7 %collective-permute-start.5 = (bf16[112,2048]{1,0:T(8,128)(2,1)S(1)}, bf16[112,2048]{1,0:T(8,128)(2,1)S(1)}, u32[]{:S(2)}, u32[]{:S(2)}) collective-permute-start(bf16[112,2048]{1,0:T(8,128)(2,1)S(1)} %collective-permute-done.3.weight_ref.w2), channel_id=1, source_target_pairs={{0,8},{8,0},{1,9},{9,1},{2,10},{10,2},{3,11},{11,3},{4,12},{12,4},... | collective-permute-start | bytes 1376264 | tf_op jit(solution)/shard_map/ppermute | solution.py:25
  116.3 1.0 copy-start.3

commit v3 on v2

v3 whole, which is shorter than its diff:
```python
import functools

import jax
import jax.numpy as jnp
from jax import lax
from jax.experimental import pallas as pl
from jax.experimental.pallas import tpu as pltpu
from jax.sharding import Mesh, PartitionSpec as P

score_scale = 192.0 ** (-0.5)
lowest = -1e30

DP = ("yh", "yl", "za", "zb", "core")
TENSOR = ("x", "zh")
SIZES = (("yh", 4), ("yl", 2), ("za", 2), ("zb", 2), ("core", 2), ("x", 4), ("zh", 2))
WIDE = ("yh", "za", "zb")
BLOCKS = ("yl", "core")

LIMIT = 16 * 1024 * 1024

VMEM = pl.BlockSpec(memory_space=pltpu.VMEM)
SMEM = pl.BlockSpec(memory_space=pltpu.SMEM)


def swap(array, axis):
    return lax.ppermute(array, axis, [(0, 1), (1, 0)])


def dot(a, b):
    return jnp.dot(a, b, preferred_element_type=jnp.float32)


def dot_rows(a, b):
    return lax.dot_general(a, b, (((1,), (1,)), ((), ())), preferred_element_type=jnp.float32)


def attend(steps, heads, width, place_ref, q0, q1, q2, q3, key_ref, fresh_ref, request_ref, out_ref):
    x, slot = place_ref[0], place_ref[2]
    lane = lax.broadcasted_iota(jnp.int32, (1, request_ref.shape[1]), 1)
    request = jnp.sum(jnp.where(lane == slot, request_ref[0:1], 0), axis=1, keepdims=True)
    limit = jnp.sum(jnp.where(lane == request, request_ref[1:2], 0), axis=1, keepdims=True)
    rows = steps * heads
    query = jnp.concatenate([q[...] for q in (q0, q1, q2, q3)], axis=0)
    fresh = fresh_ref[x]
    middle = key_ref.shape[0] // 2
    parts = [key_ref[:middle], key_ref[middle:]]
    scores = []
    for place, part in enumerate(parts):
        score = dot_rows(query, part) * score_scale
        index = lax.broadcasted_iota(jnp.int32, (1, score.shape[1]), 1)
        places = index // 8 * 16 + index % 8 // 2 * 4 + place * 2 + index % 2
        scores.append(jnp.where(places < limit, score, lowest))
    score = dot_rows(query, fresh) * score_scale
    row = lax.broadcasted_iota(jnp.int32, score.shape, 0)
    column = lax.broadcasted_iota(jnp.int32, score.shape, 1)
    scores.append(jnp.where(column <= (row % rows) // heads, score, lowest))
    top = functools.reduce(jnp.maximum, [jnp.max(score, axis=1, keepdims=True) for score in scores])
    total, summed = 0.0, 0.0
    for score, part in zip(scores, parts + [fresh]):
        raised = jnp.exp(score - top)
        total = total + jnp.sum(raised, axis=1, keepdims=True)
        summed = summed + dot(raised.astype(jnp.bfloat16), part[:, :width])
    latent = (summed / total).astype(jnp.bfloat16)
    for shift in range(4):
        out_ref[lax.rem(x + 4 - shift, 4)] = latent[shift * rows : (shift + 1) * rows]


def map_values(count, heads, latent_ref, value_ref, weight_ref, out_ref):
    latent = jnp.concatenate([latent_ref[slot] for slot in range(latent_ref.shape[0])], axis=0)
    n = latent.shape[0] // heads
    row = lax.broadcasted_iota(jnp.int32, (heads * 2 * n, 1), 0)
    head, line = row // (2 * n), row % (2 * n)
    source = jnp.where(line // n == head // (heads // 2), line % n * heads + head, -1)
    column = lax.broadcasted_iota(jnp.int32, (row.shape[0], latent.shape[0]), 1)
    pick = jnp.where(column == source, 1.0, 0.0).astype(jnp.bfloat16)
    picked = dot(pick, latent).astype(jnp.bfloat16)
    lines = out_ref.shape[1]
    half = heads // 2
    vhead = value_ref.shape[2]
    for h in range(half):
        value = dot(picked[h * lines : (h + 1) * lines], value_ref[h]) + dot(
            picked[(h + half) * lines : (h + half + 1) * lines], value_ref[h + half]
        )
        value = value.astype(jnp.bfloat16)
        for copy in range(count):
            out_ref[copy, :, h * vhead : (h + 1) * vhead] = value


def project(n, place_ref, piece_ref, own_ref, other_ref, out_ref):
    core, yl = place_ref[1], place_ref[3]
    every = piece_ref.shape[0]
    row = lax.broadcasted_iota(jnp.int32, (every, 1), 0)
    half, line = row // (every // 2), row % (every // 2)
    source = (line // n * 2 + half) * n + line % n
    column = lax.broadcasted_iota(jnp.int32, (every, every), 1)
    order = jnp.where(column == source, 1.0, 0.0).astype(jnp.bfloat16)
    lines = dot(order, piece_ref[...]).astype(jnp.bfloat16)
    rows, depth = lines.shape[0] // 2, lines.shape[1]
    groups = out_ref.shape[0] // 4
    columns = out_ref.shape[1]
    weight = jnp.concatenate([w[...] for w in (own_ref, other_ref)], axis=0)
    product = dot_rows(weight[:, :depth], lines[:rows]) + dot_rows(weight[:, depth:], lines[rows:])
    for block in range(4):
        other_y, other_core = block % 2, block // 2
        member = (1 - yl if other_y else yl) * 2 + (1 - core if other_core else core)
        for group in range(groups):
            start = (block * groups + group) * columns
            out_ref[member * groups + group] = product[start : start + columns].astype(jnp.bfloat16)


def on_device(cache, queries, new_latent, lengths, assignment, value_weight, output_weight):
    slots, steps, heads, depth = queries.shape
    requests, block = cache.shape[:2]
    width, vhead = value_weight.shape[1:]
    x_place, zh_count = lax.axis_index("x"), lax.axis_size("zh")
    groups = lax.axis_size("x") * zh_count
    rows = steps * heads

    order = (assignment[:, None] == jnp.arange(requests)[None, :]).astype(jnp.bfloat16)
    ordered = jnp.einsum(
        "jr,rpc->jpc", order, cache, preferred_element_type=jnp.float32
    ).astype(jnp.bfloat16)
    ordered = jnp.concatenate([ordered] * zh_count, axis=0)
    keys = lax.all_to_all(ordered, ("zh",) + DP + ("x",), split_axis=0, concat_axis=0, tiled=True)
    keys = keys.reshape(-1, depth)

    query = []
    for shift in range(4):
        both = lax.dynamic_index_in_dim(queries, lax.rem(x_place + shift, 4), 0, keepdims=False)
        both = both.reshape(rows, depth)
        if shift:
            both = lax.ppermute(both, "x", [(j, (j + shift) % 4) for j in range(4)])
        query.append(both)

    slot = lax.axis_index(DP) * slots + x_place
    places = jnp.stack([x_place, lax.axis_index("core"), slot, lax.axis_index("yl")]).astype(jnp.int32)
    limits = jnp.stack([assignment, lengths])
    fresh = jnp.pad(new_latent, ((0, 0), (0, 16 - steps), (0, 0)))
    weight, places, limits, fresh, keys, *query = lax.optimization_barrier(
        (output_weight.T, places, limits, fresh, keys, *query)
    )
    near_weight = swap(weight, "yl")
    latent = pl.pallas_call(
        functools.partial(attend, steps, heads, width),
        out_shape=jax.ShapeDtypeStruct((slots, rows, width), jnp.bfloat16),
        in_specs=[SMEM] + [VMEM] * 7,
        out_specs=VMEM,
        compiler_params=pltpu.CompilerParams(vmem_limit_bytes=LIMIT),
        name="attend",
    )(places, *query, keys, fresh, limits)

    latent = lax.all_to_all(latent, "x", split_axis=0, concat_axis=0, tiled=True)
    count = 1
    for axis in WIDE:
        count *= lax.axis_size(axis)
    n = slots * steps
    sent = pl.pallas_call(
        functools.partial(map_values, count, heads),
        out_shape=jax.ShapeDtypeStruct((count, 2 * n, heads // 2 * vhead), jnp.bfloat16),
        in_specs=[VMEM] * 3,
        out_specs=VMEM,
        compiler_params=pltpu.CompilerParams(vmem_limit_bytes=LIMIT),
        name="map_values",
    )(latent, value_weight, near_weight)

    sent = sent.reshape(count * 2 * n, heads // 2 * vhead)
    piece = lax.all_to_all(sent, WIDE, split_axis=0, concat_axis=0, tiled=True)
    weight = jnp.concatenate([weight, near_weight], axis=0)
    weights = (weight, swap(weight, "core"))
    own_columns = output_weight.shape[1] // groups
    product = pl.pallas_call(
        functools.partial(project, n),
        out_shape=jax.ShapeDtypeStruct((4 * groups, own_columns, count * n), jnp.bfloat16),
        in_specs=[SMEM] + [VMEM] * 3,
        out_specs=VMEM,
        compiler_params=pltpu.CompilerParams(vmem_limit_bytes=LIMIT),
        name="project",
    )(places, piece, *weights)
    terms = lax.all_to_all(product, BLOCKS + TENSOR, split_axis=0, concat_axis=0, tiled=True)
    terms = terms.reshape(4, groups, own_columns, -1)
    result = jnp.sum(terms.astype(jnp.float32), axis=1).astype(jnp.bfloat16)
    yh, yl, za, zb, core = (lax.axis_size(axis) for axis in DP)
    result = result.reshape(yl, core, own_columns, yh, za, zb, slots, steps)
    return result.transpose(3, 0, 4, 5, 1, 6, 7, 2).reshape(requests, steps, own_columns)


def solution(mesh):
    names = tuple(name for name, _ in SIZES)
    fine = Mesh(mesh.devices.reshape(tuple(size for _, size in SIZES)), names)
    return jax.shard_map(
        on_device,
        mesh=fine,
        in_specs=(
            P(None, DP + TENSOR, None),
            P(DP, None, TENSOR, None),
            P(DP, None, None),
            P(),
            P(),
            P(TENSOR, None, None),
            P(TENSOR, DP),
        ),
        out_specs=P(None, None, DP + TENSOR),
        check_vma=False,
    )
```

time: 139 us -> 136 us (0.978)
  blocking collectives: 25.5 us -> 32.1 us
  waiting for transfers between devices: 46.6 us -> 42 us
  local copies, waits for them, and re-layouts: 10.5 us -> 8.21 us
  between operations: 2.34 us -> 0.27 us
    all_to_all x1, blocking collectives: 17.9 us -> 23.5 us  [on_device(): lax.all_to_all(product, BLOCKS + TENSOR, split_axis=0, concat_axis=0, til...]
    ppermute x3, waiting for transfers between devices: 3.13 us -> 0.01 us  [on_device(): both = lax.ppermute(both, 'x', [(j, (j + shift) % 4) for j in range(4)])]
    concatenate x0 -> x2, local copies, waits for them, and re-layouts: none -> 2.83 us  [the longest x1 2.8 us: on_device(): ordered = jnp.concatenate([ordered] * zh_count, axis=0)]
    convert_element_type x1 -> x0, local copies, waits for them, and re-layouts: 2.82 us -> none  [on_device(): ordered = jnp.einsum('jr,rpc->jpc', order, cache, preferred_element_type=...]
    all_to_all x1, waiting for transfers between devices: 16.7 us -> 14 us  [on_device(): piece = lax.all_to_all(sent, WIDE, split_axis=0, concat_axis=0, tiled=True)]
    ppermute x3 -> x2, starting transfers between devices: 8.37 us -> 5.97 us  [swap(): return lax.ppermute(array, axis, [(0, 1), (1, 0)])]
    all_to_all x1, starting transfers between devices: 22.2 us -> 24 us  [on_device(): lax.all_to_all(ordered, ('zh',) + DP + ('x',), split_axis=0, concat_axis=...]
  transfers between devices with their start and end apart: 8 -> 7, of which waited for: 5 -> 3; matrix products, arithmetic and copies ran while one was open for 4% -> 3% of each run, Pallas kernels for 2% -> 1%
where the time goes in v3:
time: 136 us; the launch traced here: 135 us
  starting transfers between devices  45.9 us (34%)
  waiting for transfers between devices  42 us (31%)
  blocking collectives  32.1 us (24%)
  local copies, waits for them, and re-layouts  8.21 us (6%)
  Pallas kernels  5.6 us (4%)
    all_to_all x1, waiting for transfers between devices, on_device(): lax.all_to_all(ordered, ('zh',) + DP + ('x',), split_axis=0, concat_axis=...  25.9 us
    all_to_all x1, starting transfers between devices, on_device(): lax.all_to_all(ordered, ('zh',) + DP + ('x',), split_axis=0, concat_axis=...  24 us
    all_to_all x1, blocking collectives, on_device(): lax.all_to_all(product, BLOCKS + TENSOR, split_axis=0, concat_axis=0, til...  23.5 us
    all_to_all x1, waiting for transfers between devices, on_device(): piece = lax.all_to_all(sent, WIDE, split_axis=0, concat_axis=0, tiled=True)  14 us
    ppermute x3, starting transfers between devices, on_device(): both = lax.ppermute(both, 'x', [(j, (j + shift) % 4) for j in range(4)])  10.1 us
    all_to_all x1, blocking collectives, on_device(): lax.all_to_all(latent, 'x', split_axis=0, concat_axis=0, tiled=True)  8.63 us
    ppermute x2, starting transfers between devices, swap(): return lax.ppermute(array, axis, [(0, 1), (1, 0)])  5.97 us
    all_to_all x1, starting transfers between devices, on_device(): piece = lax.all_to_all(sent, WIDE, split_axis=0, concat_axis=0, tiled=True)  5.83 us
  transfers between devices with their start and end apart: 7, of which 3 were waited for; matrix products, arithmetic and copies ran while one was open for 3% of the time, Pallas kernels for 1%

profile of v3, /device:TPU:1, one launch (start us, length us, event | category | flops | bytes accessed | tf_op | source)
XLA Modules:
  0.0 135.4 jit_solution(17049654828758789892)
XLA Ops:
  0.0 0.0 copy-start
  0.0 1.1 copy-done
  1.1 1.1 convolution_convert_fusion
  2.2 0.1 pad_maximum_fusion
  2.3 2.8 %copy.15 = bf16[512,2,576]{2,1,0:T(2,128)(2,1)} copy(bf16[512,2,576]{0,2,1:T(8,128)(2,1)S(1)} %pad_maximum_fusion) | data formatting | bytes 2359296 | tf_op jit(solution)/shard_map/concatenate | solution.py:123
  5.1 0.0 copy-start.3
  5.1 0.0 copy-start.5
  5.1 0.0 copy-start.6
  5.1 0.0 copy-start.4
  5.1 24.0 %all-to-all-start = ((bf16[512,2,576]{2,1,0:T(2,128)(2,1)}), bf16[512,2,576]{2,1,0:T(2,128)(2,1)}, u32[]{:S(2)}, u32[]{:S(2)}) async-start(bf16[512,2,576]{2,1,0:T(2,128)(2,1)} %copy.15), calls=%async_computation | async-start | bytes 2621440 | tf_op jit(solution)/shard_map/all_to_all | solution.py:124
  29.1 0.0 copy-done.3
  29.1 3.3 %collective-permute-start = (bf16[48,576]{1,0:T(8,128)(2,1)S(1)}, bf16[48,576]{1,0:T(8,128)(2,1)S(1)}, u32[]{:S(2)}, u32[]{:S(2)}) collective-permute-start(bf16[48,576]{1,0:T(8,128)(2,1)S(1)} %bitcast.30), channel_id=1, source_target_pairs={{0,2},{2,4},{4,6},{6,0},{1,3},{3,5},{5,7},{7,1},{8,10},{10,12},{12... | collective-permute-start | bytes 165896 | tf_op jit(solution)/shard_map/ppermute | solution.py:132
  32.4 3.2 %collective-permute-start.2 = (bf16[48,576]{1,0:T(8,128)(2,1)S(1)}, bf16[48,576]{1,0:T(8,128)(2,1)S(1)}, u32[]{:S(2)}, u32[]{:S(2)}) collective-permute-start(bf16[48,576]{1,0:T(8,128)(2,1)S(1)} %bitcast.29), channel_id=1, source_target_pairs={{0,6},{2,0},{4,2},{6,4},{1,7},{3,1},{5,3},{7,5},{8,14},{10,8},{12,... | collective-permute-start | bytes 165896 | tf_op jit(solution)/shard_map/ppermute | solution.py:132
  35.6 3.6 %collective-permute-start.1 = (bf16[48,576]{1,0:T(8,128)(2,1)S(1)}, bf16[48,576]{1,0:T(8,128)(2,1)S(1)}, u32[]{:S(2)}, u32[]{:S(2)}) collective-permute-start(bf16[48,576]{1,0:T(8,128)(2,1)S(1)} %bitcast.28), channel_id=1, source_target_pairs={{0,4},{2,6},{4,0},{6,2},{1,5},{3,7},{5,1},{7,3},{8,12},{10,14},{12... | collective-permute-start | bytes 165896 | tf_op jit(solution)/shard_map/ppermute | solution.py:132
  39.3 0.0 copy-done.5
  39.3 0.0 copy-done.6
  39.3 0.1 pad_add_fusion.1.place_ref
  39.4 0.0 copy-done.4
  39.4 25.9 %all-to-all-done = bf16[512,2,576]{2,1,0:T(2,128)(2,1)} async-done(((bf16[512,2,576]{2,1,0:T(2,128)(2,1)}), bf16[512,2,576]{2,1,0:T(2,128)(2,1)}, u32[]{:S(2)}, u32[]{:S(2)}) %all-to-all-start) | async-done | bytes 1179680 | tf_op jit(solution)/shard_map/all_to_all | solution.py:124
  65.3 3.2 %reshape.33.key_ref = bf16[1024,576]{1,0:T(8,128)(2,1)S(1)} reshape(bf16[512,2,576]{2,1,0:T(2,128)(2,1)} %all-to-all-done) | data formatting | bytes 2359296 | tf_op jit(solution)/shard_map/reshape | solution.py:125
  68.5 0.0 copy-start.1
  68.5 0.0 collective-permute-done.q1
  68.6 0.0 collective-permute-done.2.q3
  68.6 0.0 collective-permute-done.1.q2
  68.6 2.3 %collective-permute-start.3 = (bf16[112,2048]{1,0:T(8,128)(2,1)}, bf16[112,2048]{1,0:T(8,128)(2,1)S(1)}, u32[]{:S(2)}, u32[]{:S(2)}) collective-permute-start(bf16[112,2048]{1,0:T(8,128)(2,1)} %bitcast.26), channel_id=1, source_target_pairs={{0,64},{64,0},{1,65},{65,1},{2,66},{66,2},{3,67},{67,3},{4,68},{68... | collective-permute-start | bytes 1376264 | tf_op jit(solution)/shard_map/ppermute | solution.py:26
  70.9 1.7 %attend.1 = bf16[4,48,512]{2,1,0:T(8,128)(2,1)S(1)} custom-call(s32[4]{0:T(128)S(1)} %pad_add_fusion.1.place_ref, bf16[48,576]{1,0:T(8,128)(2,1)S(1)} %bitcast.23, bf16[48,576]{1,0:T(8,128)(2,1)S(1)} %collective-permute-done.q1, bf16[48,576]{1,0:T(8,128)(2,1)S(1)} %collective-permute-done.1.q2, bf16[48,576]{1,0:T(8,128)(2,1)S(1)} %collective-permute-done.2.q3, ...), custom_call_target="tpu_custom_call" | custom-call | tf_op jit(solution)/shard_map/attend/pallas_call | solution.py:143
  72.6 8.6 %all_to_all.23.latent_ref = bf16[4,48,512]{2,1,0:T(8,128)(2,1)S(1)} all-to-all(bf16[4,48,512]{2,1,0:T(8,128)(2,1)S(1)} %attend.1), channel_id=1, replica_groups=mesh['yh'=4,'yl'=2,'za'=2,'zb'=2,'core'=2,'x'=4,'zh'=2] {'x'}, dimensions={0} | all-to-all | bytes 393216 | tf_op jit(solution)/shard_map/all_to_all | solution.py:152
  81.2 0.0 collective-permute-done.3.weight_ref
  81.2 0.0 copy-done.1
  81.2 1.8 %map_values.1 = bf16[16,24,1024]{2,1,0:T(8,128)(2,1)} custom-call(bf16[4,48,512]{2,1,0:T(8,128)(2,1)S(1)} %all_to_all.23.latent_ref, bf16[16,512,128]{2,1,0:T(8,128)(2,1)S(1)} %copy-done.1, bf16[112,2048]{1,0:T(8,128)(2,1)S(1)} %collective-permute-done.3.weight_ref), custom_call_target="tpu_custom_call" | custom-call | tf_op jit(solution)/shard_map/map_values/pallas_call | solution.py:157
  83.0 0.0 copy-start.2
  83.0 5.8 %all-to-all-start.2 = ((bf16[16,24,1024]{2,1,0:T(8,128)(2,1)}), bf16[16,24,1024]{2,1,0:T(8,128)(2,1)S(1)}, u32[]{:S(2)}, u32[]{:S(2)}) async-start(bf16[16,24,1024]{2,1,0:T(8,128)(2,1)} %map_values.1), calls=%async_computation.2 | async-start | bytes 1572864 | tf_op jit(solution)/shard_map/all_to_all | solution.py:167
  88.8 0.0 copy-done.2
  88.9 3.7 %collective-permute-start.4 = (bf16[224,2048]{1,0:T(8,128)(2,1)S(1)}, bf16[224,2048]{1,0:T(8,128)(2,1)S(1)}, u32[]{:S(2)}, u32[]{:S(2)}) collective-permute-start(bf16[224,2048]{1,0:T(8,128)(2,1)S(1)} %constant_dynamic-update-slice_fusion.own_ref), channel_id=1, source_target_pairs={{0,8},{8,0},{1,9},{9,1},{2,10},{10,2},{3,11},{11,3},{4,12},{12,4},... | collective-permute-start | bytes 2752520 | tf_op jit(solution)/shard_map/ppermute | solution.py:26
  92.6 2.1 %collective-permute-done.4.other_ref = bf16[224,2048]{1,0:T(8,128)(2,1)S(1)} collective-permute-done((bf16[224,2048]{1,0:T(8,128)(2,1)S(1)}, bf16[224,2048]{1,0:T(8,128)(2,1)S(1)}, u32[]{:S(2)}, u32[]{:S(2)}) %collective-permute-start.4) | collective-permute-done | bytes 917536 | tf_op jit(solution)/shard_map/ppermute | solution.py:26
  94.7 14.0 %all-to-all-done.2 = bf16[16,24,1024]{2,1,0:T(8,128)(2,1)S(1)} async-done(((bf16[16,24,1024]{2,1,0:T(8,128)(2,1)}), bf16[16,24,1024]{2,1,0:T(8,128)(2,1)S(1)}, u32[]{:S(2)}, u32[]{:S(2)}) %all-to-all-start.2) | async-done | bytes 786464 | tf_op jit(solution)/shard_map/all_to_all | solution.py:167
  108.7 2.1 %project.1 = bf16[32,14,192]{2,1,0:T(8,128)(2,1)S(1)} custom-call(s32[4]{0:T(128)S(1)} %pad_add_fusion.1.place_ref, bf16[384,1024]{1,0:T(8,128)(2,1)S(1)} %bitcast.22, bf16[224,2048]{1,0:T(8,128)(2,1)S(1)} %constant_dynamic-update-slice_fusion.own_ref, bf16[224,2048]{1,0:T(8,128)(2,1)S(1)} %collective-permute-done.4.other_ref), custom_call_target="tpu_custom_call" | custom-call | tf_op jit(solution)/shard_map/project/pallas_call | solution.py:171
  110.8 23.5 %all_to_all.24 = bf16[32,14,192]{2,1,0:T(8,128)(2,1)S(1)} all-to-all(bf16[32,14,192]{2,1,0:T(8,128)(2,1)S(1)} %project.1), channel_id=1, replica_groups=mesh['yh'=4,'yl'=2,'za'=2,'zb'=2,'core'=2,'x'=4,'zh'=2] {'yl','core','x'..., dimensions={0} | all-to-all | bytes 344064 | tf_op jit(solution)/shard_map/all_to_all | solution.py:179
  134.3 0.1 bitcast_reduce_fusion
  134.3 0.2 copy.16
  134.5 0.1 copy.17
  134.6 0.7 copy.18
  (6 shorter events, 0.1 us)
Async XLA Ops:
  0.0 1.1 copy-start
  5.1 24.0 %copy-start.3 = (bf16[4,3,16,576]{3,2,1,0:T(8,128)(2,1)S(1)}, bf16[4,3,16,576]{3,2,1,0:T(8,128)(2,1)}, u32[]{:S(2)}) copy-start(bf16[4,3,16,576]{3,2,1,0:T(8,128)(2,1)} %param.8) | copy-start | bytes 663556
  5.1 34.2 %copy-start.5 = (s32[256]{0:T(256)S(1)}, s32[256]{0:T(256)}, u32[]{:S(2)}) copy-start(s32[256]{0:T(256)} %param.11) | copy-start | bytes 3076
  5.1 34.2 %copy-start.6 = (s32[256]{0:T(256)S(1)}, s32[256]{0:T(256)}, u32[]{:S(2)}) copy-start(s32[256]{0:T(256)} %param.10) | copy-start | bytes 3076
  5.1 34.3 %copy-start.4 = (bf16[4,3,576]{2,0,1:T(4,128)(2,1)S(1)}, bf16[4,3,576]{2,0,1:T(4,128)(2,1)}, u32[]{:S(2)}) copy-start(bf16[4,3,576]{2,0,1:T(4,128)(2,1)} %param.9) | copy-start | bytes 41476
  5.1 60.3 %all-to-all-start = ((bf16[512,2,576]{2,1,0:T(2,128)(2,1)}), bf16[512,2,576]{2,1,0:T(2,128)(2,1)}, u32[]{:S(2)}, u32[]{:S(2)}) async-start(bf16[512,2,576]{2,1,0:T(2,128)(2,1)} %copy.15), calls=%async_computation | async-start | bytes 2621440 | tf_op jit(solution)/shard_map/all_to_all | solution.py:124
  29.1 39.4 %collective-permute-start = (bf16[48,576]{1,0:T(8,128)(2,1)S(1)}, bf16[48,576]{1,0:T(8,128)(2,1)S(1)}, u32[]{:S(2)}, u32[]{:S(2)}) collective-permute-start(bf16[48,576]{1,0:T(8,128)(2,1)S(1)} %bitcast.30), channel_id=1, source_target_pairs={{0,2},{2,4},{4,6},{6,0},{1,3},{3,5},{5,7},{7,1},{8,10},{10,12},{12... | collective-permute-start | bytes 165896 | tf_op jit(solution)/shard_map/ppermute | solution.py:132
  32.4 36.1 %collective-permute-start.2 = (bf16[48,576]{1,0:T(8,128)(2,1)S(1)}, bf16[48,576]{1,0:T(8,128)(2,1)S(1)}, u32[]{:S(2)}, u32[]{:S(2)}) collective-permute-start(bf16[48,576]{1,0:T(8,128)(2,1)S(1)} %bitcast.29), channel_id=1, source_target_pairs={{0,6},{2,0},{4,2},{6,4},{1,7},{3,1},{5,3},{7,5},{8,14},{10,8},{12,... | collective-permute-start | bytes 165896 | tf_op jit(solution)/shard_map/ppermute | solution.py:132
  35.6 32.9 %collective-permute-start.1 = (bf16[48,576]{1,0:T(8,128)(2,1)S(1)}, bf16[48,576]{1,0:T(8,128)(2,1)S(1)}, u32[]{:S(2)}, u32[]{:S(2)}) collective-permute-start(bf16[48,576]{1,0:T(8,128)(2,1)S(1)} %bitcast.28), channel_id=1, source_target_pairs={{0,4},{2,6},{4,0},{6,2},{1,5},{3,7},{5,1},{7,3},{8,12},{10,14},{12... | collective-permute-start | bytes 165896 | tf_op jit(solution)/shard_map/ppermute | solution.py:132
  68.5 12.7 %copy-start.1 = (bf16[16,512,128]{2,1,0:T(8,128)(2,1)S(1)}, bf16[16,512,128]{2,1,0:T(8,128)(2,1)}, u32[]{:S(2)}) copy-start(bf16[16,512,128]{2,1,0:T(8,128)(2,1)} %value_ref.1) | copy-start | bytes 6291460
  68.6 12.6 %collective-permute-start.3 = (bf16[112,2048]{1,0:T(8,128)(2,1)}, bf16[112,2048]{1,0:T(8,128)(2,1)S(1)}, u32[]{:S(2)}, u32[]{:S(2)}) collective-permute-start(bf16[112,2048]{1,0:T(8,128)(2,1)} %bitcast.26), channel_id=1, source_target_pairs={{0,64},{64,0},{1,65},{65,1},{2,66},{66,2},{3,67},{67,3},{4,68},{68... | collective-permute-start | bytes 1376264 | tf_op jit(solution)/shard_map/ppermute | solution.py:26
  83.0 5.8 %copy-start.2 = (bf16[2048,112]{0,1:T(8,128)(2,1)S(1)}, bf16[2048,112]{0,1:T(8,128)(2,1)}, u32[]{:S(2)}) copy-start(bf16[2048,112]{0,1:T(8,128)(2,1)} %param.13) | copy-start | bytes 1376260
  83.0 25.7 %all-to-all-start.2 = ((bf16[16,24,1024]{2,1,0:T(8,128)(2,1)}), bf16[16,24,1024]{2,1,0:T(8,128)(2,1)S(1)}, u32[]{:S(2)}, u32[]{:S(2)}) async-start(bf16[16,24,1024]{2,1,0:T(8,128)(2,1)} %map_values.1), calls=%async_computation.2 | async-start | bytes 1572864 | tf_op jit(solution)/shard_map/all_to_all | solution.py:167
  88.9 5.8 %collective-permute-start.4 = (bf16[224,2048]{1,0:T(8,128)(2,1)S(1)}, bf16[224,2048]{1,0:T(8,128)(2,1)S(1)}, u32[]{:S(2)}, u32[]{:S(2)}) collective-permute-start(bf16[224,2048]{1,0:T(8,128)(2,1)S(1)} %constant_dynamic-update-slice_fusion.own_ref), channel_id=1, source_target_pairs={{0,8},{8,0},{1,9},{9,1},{2,10},{10,2},{3,11},{11,3},{4,12},{12,4},... | collective-permute-start | bytes 2752520 | tf_op jit(solution)/shard_map/ppermute | solution.py:26

commit v4 on v3

--- a/solution.py
+++ b/solution.py
@@ -13,8 +13,8 @@
 DP = ("yh", "yl", "za", "zb", "core")
 TENSOR = ("x", "zh")
 SIZES = (("yh", 4), ("yl", 2), ("za", 2), ("zb", 2), ("core", 2), ("x", 4), ("zh", 2))
-WIDE = ("yh", "za", "zb")
-BLOCKS = ("yl", "core")
+WIDE = ("yh", "za")
+BLOCKS = ("yl", "zb", "core")
 
 LIMIT = 16 * 1024 * 1024
 
@@ -65,7 +65,7 @@
         out_ref[lax.rem(x + 4 - shift, 4)] = latent[shift * rows : (shift + 1) * rows]
 
 
-def map_values(count, heads, latent_ref, value_ref, weight_ref, out_ref):
+def map_values(count, heads, latent_ref, value_ref, out_ref):
     latent = jnp.concatenate([latent_ref[slot] for slot in range(latent_ref.shape[0])], axis=0)
     n = latent.shape[0] // heads
     row = lax.broadcasted_iota(jnp.int32, (heads * 2 * n, 1), 0)
@@ -87,7 +87,7 @@
 
 
 def project(n, place_ref, piece_ref, own_ref, other_ref, out_ref):
-    core, yl = place_ref[1], place_ref[3]
+    core, yl, zb = place_ref[1], place_ref[3], place_ref[4]
     every = piece_ref.shape[0]
     row = lax.broadcasted_iota(jnp.int32, (every, 1), 0)
     half, line = row // (every // 2), row % (every // 2)
@@ -96,13 +96,14 @@
     order = jnp.where(column == source, 1.0, 0.0).astype(jnp.bfloat16)
     lines = dot(order, piece_ref[...]).astype(jnp.bfloat16)
     rows, depth = lines.shape[0] // 2, lines.shape[1]
-    groups = out_ref.shape[0] // 4
+    groups = out_ref.shape[0] // 8
     columns = out_ref.shape[1]
     weight = jnp.concatenate([w[...] for w in (own_ref, other_ref)], axis=0)
     product = dot_rows(weight[:, :depth], lines[:rows]) + dot_rows(weight[:, depth:], lines[rows:])
-    for block in range(4):
-        other_y, other_core = block % 2, block // 2
-        member = (1 - yl if other_y else yl) * 2 + (1 - core if other_core else core)
+    for block in range(8):
+        other_core, other_y, other_z = block // 4, block // 2 % 2, block % 2
+        member = (1 - yl if other_y else yl) * 2 + (1 - zb if other_z else zb)
+        member = member * 2 + (1 - core if other_core else core)
         for group in range(groups):
             start = (block * groups + group) * columns
             out_ref[member * groups + group] = product[start : start + columns].astype(jnp.bfloat16)
@@ -133,13 +134,15 @@
         query.append(both)
 
     slot = lax.axis_index(DP) * slots + x_place
-    places = jnp.stack([x_place, lax.axis_index("core"), slot, lax.axis_index("yl")]).astype(jnp.int32)
+    places = jnp.stack([x_place, lax.axis_index("core"), slot, lax.axis_index("yl"), lax.axis_index("zb")]).astype(jnp.int32)
     limits = jnp.stack([assignment, lengths])
     fresh = jnp.pad(new_latent, ((0, 0), (0, 16 - steps), (0, 0)))
-    weight, places, limits, fresh, keys, *query = lax.optimization_barrier(
-        (output_weight.T, places, limits, fresh, keys, *query)
+    weight, places, limits, fresh, *query = lax.optimization_barrier(
+        (output_weight.T, places, limits, fresh, *query)
     )
-    near_weight = swap(weight, "yl")
+    near_weights = [
+        lax.ppermute(weight, ("yl", "zb"), [(j, j ^ step) for j in range(4)]) for step in (1, 2, 3)
+    ]
     latent = pl.pallas_call(
         functools.partial(attend, steps, heads, width),
         out_shape=jax.ShapeDtypeStruct((slots, rows, width), jnp.bfloat16),
@@ -157,31 +160,32 @@
     sent = pl.pallas_call(
         functools.partial(map_values, count, heads),
         out_shape=jax.ShapeDtypeStruct((count, 2 * n, heads // 2 * vhead), jnp.bfloat16),
-        in_specs=[VMEM] * 3,
+        in_specs=[VMEM] * 2,
         out_specs=VMEM,
         compiler_params=pltpu.CompilerParams(vmem_limit_bytes=LIMIT),
         name="map_values",
-    )(latent, value_weight, near_weight)
+    )(latent, value_weight)
 
     sent = sent.reshape(count * 2 * n, heads // 2 * vhead)
+    sent, *near_weights = lax.optimization_barrier((sent, *near_weights))
     piece = lax.all_to_all(sent, WIDE, split_axis=0, concat_axis=0, tiled=True)
-    weight = jnp.concatenate([weight, near_weight], axis=0)
+    weight = jnp.concatenate([weight, *near_weights], axis=0)
     weights = (weight, swap(weight, "core"))
     own_columns = output_weight.shape[1] // groups
     product = pl.pallas_call(
         functools.partial(project, n),
-        out_shape=jax.ShapeDtypeStruct((4 * groups, own_columns, count * n), jnp.bfloat16),
+        out_shape=jax.ShapeDtypeStruct((8 * groups, own_columns, count * n), jnp.bfloat16),
         in_specs=[SMEM] + [VMEM] * 3,
         out_specs=VMEM,
         compiler_params=pltpu.CompilerParams(vmem_limit_bytes=LIMIT),
         name="project",
     )(places, piece, *weights)
     terms = lax.all_to_all(product, BLOCKS + TENSOR, split_axis=0, concat_axis=0, tiled=True)
-    terms = terms.reshape(4, groups, own_columns, -1)
+    terms = terms.reshape(8, groups, own_columns, -1)
     result = jnp.sum(terms.astype(jnp.float32), axis=1).astype(jnp.bfloat16)
     yh, yl, za, zb, core = (lax.axis_size(axis) for axis in DP)
-    result = result.reshape(yl, core, own_columns, yh, za, zb, slots, steps)
-    return result.transpose(3, 0, 4, 5, 1, 6, 7, 2).reshape(requests, steps, own_columns)
+    result = result.reshape(yl, zb, core, own_columns, yh, za, slots, steps)
+    return result.transpose(4, 0, 5, 1, 2, 6, 7, 3).reshape(requests, steps, own_columns)
 
 
 def solution(mesh):

time: 136 us -> 131 us (0.963)
  waiting for transfers between devices: 42 us -> 23.2 us
  blocking collectives: 32.1 us -> 38.1 us
  starting transfers between devices: 45.9 us -> 50.7 us
  local copies, waits for them, and re-layouts: 8.21 us -> 12 us
    all_to_all x1, waiting for transfers between devices: 25.9 us -> 14.4 us  [on_device(): lax.all_to_all(ordered, ('zh',) + DP + ('x',), split_axis=0, concat_axis=...]
    all_to_all x1, waiting for transfers between devices: 14 us -> 5.1 us  [on_device(): lax.all_to_all(latent, 'x', split_axis=0, concat_axis=0, tiled=True)]
    ppermute x0 -> x3, starting transfers between devices: none -> 8.77 us  [on_device(): lax.ppermute(weight, ('yl', 'zb'), [(j, j ^ step) for j in range(4)])]
    all_to_all x1, blocking collectives: 8.63 us -> 16.9 us  [on_device(): piece = lax.all_to_all(sent, WIDE, split_axis=0, concat_axis=0, tiled=True)]
    unnamed x16 -> x18, local copies, waits for them, and re-layouts: 1.13 us -> 4.82 us
    ppermute x3, waiting for transfers between devices: 0.01 us -> 3.69 us  [on_device(): both = lax.ppermute(both, 'x', [(j, (j + shift) % 4) for j in range(4)])]
    all_to_all x1, starting transfers between devices: 5.83 us -> 3.36 us  [on_device(): lax.all_to_all(latent, 'x', split_axis=0, concat_axis=0, tiled=True)]
    all_to_all x1, blocking collectives: 23.5 us -> 21.2 us  [on_device(): lax.all_to_all(product, BLOCKS + TENSOR, split_axis=0, concat_axis=0, til...]
  transfers between devices with their start and end apart: 7 -> 9, of which waited for: 3 -> 3; matrix products, arithmetic and copies ran while one was open for 3% -> 3% of each run, Pallas kernels for 1% -> 2%
where the time goes in v4:
time: 131 us
  starting transfers between devices  50.7 us (39%)
  blocking collectives  38.1 us (29%)
  waiting for transfers between devices  23.2 us (18%)
  local copies, waits for them, and re-layouts  12 us (9%)
  Pallas kernels  5.1 us (4%)
    all_to_all x1, starting transfers between devices, on_device(): lax.all_to_all(ordered, ('zh',) + DP + ('x',), split_axis=0, concat_axis=...  24 us
    all_to_all x1, blocking collectives, on_device(): lax.all_to_all(product, BLOCKS + TENSOR, split_axis=0, concat_axis=0, til...  21.2 us
    all_to_all x1, blocking collectives, on_device(): piece = lax.all_to_all(sent, WIDE, split_axis=0, concat_axis=0, tiled=True)  16.9 us
    all_to_all x1, waiting for transfers between devices, on_device(): lax.all_to_all(ordered, ('zh',) + DP + ('x',), split_axis=0, concat_axis=...  14.4 us
    ppermute x3, starting transfers between devices, on_device(): both = lax.ppermute(both, 'x', [(j, (j + shift) % 4) for j in range(4)])  10.1 us
    ppermute x3, starting transfers between devices, on_device(): lax.ppermute(weight, ('yl', 'zb'), [(j, j ^ step) for j in range(4)])  8.77 us
    all_to_all x1, waiting for transfers between devices, on_device(): lax.all_to_all(latent, 'x', split_axis=0, concat_axis=0, tiled=True)  5.1 us
    unnamed x18, local copies, waits for them, and re-layouts  4.82 us
  transfers between devices with their start and end apart: 9, of which 3 were waited for; matrix products, arithmetic and copies ran while one was open for 3% of the time, Pallas kernels for 2%

profile of v4, /device:TPU:1, one launch (start us, length us, event | category | flops | bytes accessed | tf_op | source)
XLA Modules:
  0.0 130.6 jit_solution(16400261746111342930)
XLA Ops:
  0.0 0.0 copy-start
  0.0 1.1 copy-done
  1.1 1.1 convolution_convert_fusion
  2.2 0.1 pad_maximum_fusion
  2.3 2.8 %copy.15 = bf16[512,2,576]{2,1,0:T(2,128)(2,1)} copy(bf16[512,2,576]{0,2,1:T(8,128)(2,1)S(1)} %pad_maximum_fusion) | data formatting | bytes 2359296 | tf_op jit(solution)/shard_map/concatenate | solution.py:124
  5.1 0.0 copy-start.3
  5.1 0.0 copy-start.5
  5.1 0.0 copy-start.6
  5.1 0.0 copy-start.4
  5.1 0.0 copy-start.2
  5.1 24.0 %all-to-all-start = ((bf16[512,2,576]{2,1,0:T(2,128)(2,1)}), bf16[512,2,576]{2,1,0:T(2,128)(2,1)}, u32[]{:S(2)}, u32[]{:S(2)}) async-start(bf16[512,2,576]{2,1,0:T(2,128)(2,1)} %copy.15), calls=%async_computation | async-start | bytes 2621440 | tf_op jit(solution)/shard_map/all_to_all | solution.py:125
  29.1 0.0 copy-done.3
  29.2 3.3 %collective-permute-start = (bf16[48,576]{1,0:T(8,128)(2,1)S(1)}, bf16[48,576]{1,0:T(8,128)(2,1)S(1)}, u32[]{:S(2)}, u32[]{:S(2)}) collective-permute-start(bf16[48,576]{1,0:T(8,128)(2,1)S(1)} %bitcast.35), channel_id=1, source_target_pairs={{0,2},{2,4},{4,6},{6,0},{1,3},{3,5},{5,7},{7,1},{8,10},{10,12},{12... | collective-permute-start | bytes 165896 | tf_op jit(solution)/shard_map/ppermute | solution.py:133
  32.5 3.2 %collective-permute-start.2 = (bf16[48,576]{1,0:T(8,128)(2,1)S(1)}, bf16[48,576]{1,0:T(8,128)(2,1)S(1)}, u32[]{:S(2)}, u32[]{:S(2)}) collective-permute-start(bf16[48,576]{1,0:T(8,128)(2,1)S(1)} %bitcast.34), channel_id=1, source_target_pairs={{0,6},{2,0},{4,2},{6,4},{1,7},{3,1},{5,3},{7,5},{8,14},{10,8},{12,... | collective-permute-start | bytes 165896 | tf_op jit(solution)/shard_map/ppermute | solution.py:133
  35.7 3.6 %collective-permute-start.1 = (bf16[48,576]{1,0:T(8,128)(2,1)S(1)}, bf16[48,576]{1,0:T(8,128)(2,1)S(1)}, u32[]{:S(2)}, u32[]{:S(2)}) collective-permute-start(bf16[48,576]{1,0:T(8,128)(2,1)S(1)} %bitcast.33), channel_id=1, source_target_pairs={{0,4},{2,6},{4,0},{6,2},{1,5},{3,7},{5,1},{7,3},{8,12},{10,14},{12... | collective-permute-start | bytes 165896 | tf_op jit(solution)/shard_map/ppermute | solution.py:133
  39.3 0.0 copy-done.5
  39.3 0.0 copy-done.6
  39.3 0.0 copy-done.4
  39.4 0.1 stack.32.place_ref
  39.4 0.0 collective-permute-done.q1
  39.5 0.0 collective-permute-done.2.q3
  39.5 3.7 %collective-permute-done.1.q2 = bf16[48,576]{1,0:T(8,128)(2,1)S(1)} collective-permute-done((bf16[48,576]{1,0:T(8,128)(2,1)S(1)}, bf16[48,576]{1,0:T(8,128)(2,1)S(1)}, u32[]{:S(2)}, u32[]{:S(2)}) %collective-permute-start.1) | collective-permute-done | bytes 55328 | tf_op jit(solution)/shard_map/ppermute | solution.py:133
  43.1 0.0 copy-done.2
  43.1 4.6 %collective-permute-start.5 = (bf16[112,2048]{1,0:T(8,128)(2,1)S(1)}, bf16[112,2048]{1,0:T(8,128)(2,1)S(1)}, u32[]{:S(2)}, u32[]{:S(2)}) collective-permute-start(bf16[112,2048]{1,0:T(8,128)(2,1)S(1)} %bitcast.29), channel_id=1, source_target_pairs={{0,80},{16,64},{64,16},{80,0},{1,81},{17,65},{65,17},{81,1},{2,82}... | collective-permute-start | bytes 1376264 | tf_op jit(solution)/shard_map/ppermute | solution.py:144
  47.8 2.2 %collective-permute-start.4 = (bf16[112,2048]{1,0:T(8,128)(2,1)S(1)}, bf16[112,2048]{1,0:T(8,128)(2,1)}, u32[]{:S(2)}, u32[]{:S(2)}) collective-permute-start(bf16[112,2048]{1,0:T(8,128)(2,1)S(1)} %bitcast.30), channel_id=1, source_target_pairs={{0,64},{16,80},{64,0},{80,16},{1,65},{17,81},{65,1},{81,17},{2,66}... | collective-permute-start | bytes 1376264 | tf_op jit(solution)/shard_map/ppermute | solution.py:144
  50.0 1.9 %collective-permute-start.3 = (bf16[112,2048]{1,0:T(8,128)(2,1)S(1)}, bf16[112,2048]{1,0:T(8,128)(2,1)}, u32[]{:S(2)}, u32[]{:S(2)}) collective-permute-start(bf16[112,2048]{1,0:T(8,128)(2,1)S(1)} %bitcast.31), channel_id=1, source_target_pairs={{0,16},{16,0},{64,80},{80,64},{1,17},{17,1},{65,81},{81,65},{2,18}... | collective-permute-start | bytes 1376264 | tf_op jit(solution)/shard_map/ppermute | solution.py:144
  51.9 14.4 %all-to-all-done = bf16[512,2,576]{2,1,0:T(2,128)(2,1)} async-done(((bf16[512,2,576]{2,1,0:T(2,128)(2,1)}), bf16[512,2,576]{2,1,0:T(2,128)(2,1)}, u32[]{:S(2)}, u32[]{:S(2)}) %all-to-all-start) | async-done | bytes 1179680 | tf_op jit(solution)/shard_map/all_to_all | solution.py:125
  66.3 3.2 %reshape.38.key_ref = bf16[1024,576]{1,0:T(8,128)(2,1)S(1)} reshape(bf16[512,2,576]{2,1,0:T(2,128)(2,1)} %all-to-all-done) | data formatting | bytes 2359296 | tf_op jit(solution)/shard_map/reshape | solution.py:126
  69.5 2.4 %attend.1 = bf16[4,48,512]{2,1,0:T(8,128)(2,1)} custom-call(s32[5]{0:T(128)S(1)} %stack.32.place_ref, bf16[48,576]{1,0:T(8,128)(2,1)S(1)} %bitcast.26, bf16[48,576]{1,0:T(8,128)(2,1)S(1)} %collective-permute-done.q1, bf16[48,576]{1,0:T(8,128)(2,1)S(1)} %collective-permute-done.1.q2, bf16[48,576]{1,0:T(8,128)(2,1)S(1)} %collective-permute-done.2.q3, ...), custom_call_target="tpu_custom_call" | custom-call | tf_op jit(solution)/shard_map/attend/pallas_call | solution.py:146
  71.9 3.4 %all-to-all-start.1 = ((bf16[4,48,512]{2,1,0:T(8,128)(2,1)}), bf16[4,48,512]{2,1,0:T(8,128)(2,1)S(1)}, u32[]{:S(2)}, u32[]{:S(2)}) async-start(bf16[4,48,512]{2,1,0:T(8,128)(2,1)} %attend.1), calls=%async_computation.1 | async-start | bytes 393216 | tf_op jit(solution)/shard_map/all_to_all | solution.py:155
  75.3 5.1 %all-to-all-done.1.latent_ref = bf16[4,48,512]{2,1,0:T(8,128)(2,1)S(1)} async-done(((bf16[4,48,512]{2,1,0:T(8,128)(2,1)}), bf16[4,48,512]{2,1,0:T(8,128)(2,1)S(1)}, u32[]{:S(2)}, u32[]{:S(2)}) %all-to-all-start.1) | async-done | bytes 196640 | tf_op jit(solution)/shard_map/all_to_all | solution.py:155
  80.4 0.0 copy-start.1
  80.4 1.6 %copy-done.1 = bf16[16,512,128]{2,1,0:T(8,128)(2,1)S(1)} copy-done((bf16[16,512,128]{2,1,0:T(8,128)(2,1)S(1)}, bf16[16,512,128]{2,1,0:T(8,128)(2,1)}, u32[]{:S(2)}) %copy-start.1) | copy-done | bytes 2097176
  82.0 0.8 map_values.1
  82.8 0.0 collective-permute-done.5
  82.8 0.0 collective-permute-done.4
  82.8 0.0 collective-permute-done.3
  82.8 1.1 constant_dynamic-update-slice_fusion.2
  83.9 1.1 constant_dynamic-update-slice_fusion.1
  85.0 4.5 %collective-permute-start.6 = (bf16[448,2048]{1,0:T(8,128)(2,1)S(1)}, bf16[448,2048]{1,0:T(8,128)(2,1)S(1)}, u32[]{:S(2)}, u32[]{:S(2)}) collective-permute-start(bf16[448,2048]{1,0:T(8,128)(2,1)S(1)} %constant_dynamic-update-slice_fusion.own_ref), channel_id=1, source_target_pairs={{0,8},{8,0},{1,9},{9,1},{2,10},{10,2},{3,11},{11,3},{4,12},{12,4},... | collective-permute-start | bytes 5505032 | tf_op jit(solution)/shard_map/ppermute | solution.py:26
  89.5 16.9 %all_to_all.26 = bf16[8,24,1024]{2,1,0:T(8,128)(2,1)S(1)} all-to-all(bf16[8,24,1024]{2,1,0:T(8,128)(2,1)S(1)} %map_values.1), channel_id=1, replica_groups=mesh['yh'=4,'yl'=2,'za'=2,'zb'=2,'core'=2,'x'=4,'zh'=2] {'yh','za'}, dimensions={0} | all-to-all | bytes 786432 | tf_op jit(solution)/shard_map/all_to_all | solution.py:171
  106.4 0.0 collective-permute-done.6.other_ref
  106.4 1.9 %project.1 = bf16[64,14,96]{2,1,0:T(8,128)(2,1)S(1)} custom-call(s32[5]{0:T(128)S(1)} %stack.32.place_ref, bf16[192,1024]{1,0:T(8,128)(2,1)S(1)} %bitcast.25, bf16[448,2048]{1,0:T(8,128)(2,1)S(1)} %constant_dynamic-update-slice_fusion.own_ref, bf16[448,2048]{1,0:T(8,128)(2,1)S(1)} %collective-permute-done.6.other_ref), custom_call_target="tpu_custom_call" | custom-call | tf_op jit(solution)/shard_map/project/pallas_call | solution.py:175
  108.3 21.2 %all_to_all.27 = bf16[64,14,96]{2,1,0:T(8,128)(2,1)S(1)} all-to-all(bf16[64,14,96]{2,1,0:T(8,128)(2,1)S(1)} %project.1), channel_id=1, replica_groups=mesh['yh'=4,'yl'=2,'za'=2,'zb'=2,'core'=2,'x'=4,'zh'=2] {'yl','zb','core..., dimensions={0} | all-to-all | bytes 344064 | tf_op jit(solution)/shard_map/all_to_all | solution.py:183
  129.5 0.1 bitcast_reduce_fusion
  129.5 0.2 copy.16
  129.7 0.1 copy.17
  129.8 0.7 copy.18
  (6 shorter events, 0.1 us)
Async XLA Ops:
  0.0 1.1 copy-start
  5.1 24.0 %copy-start.3 = (bf16[4,3,16,576]{3,2,1,0:T(8,128)(2,1)S(1)}, bf16[4,3,16,576]{3,2,1,0:T(8,128)(2,1)}, u32[]{:S(2)}) copy-start(bf16[4,3,16,576]{3,2,1,0:T(8,128)(2,1)} %param.8) | copy-start | bytes 663556
  5.1 34.2 %copy-start.5 = (s32[256]{0:T(256)S(1)}, s32[256]{0:T(256)}, u32[]{:S(2)}) copy-start(s32[256]{0:T(256)} %param.11) | copy-start | bytes 3076
  5.1 34.2 %copy-start.6 = (s32[256]{0:T(256)S(1)}, s32[256]{0:T(256)}, u32[]{:S(2)}) copy-start(s32[256]{0:T(256)} %param.10) | copy-start | bytes 3076
  5.1 34.2 %copy-start.4 = (bf16[4,3,576]{2,0,1:T(4,128)(2,1)S(1)}, bf16[4,3,576]{2,0,1:T(4,128)(2,1)}, u32[]{:S(2)}) copy-start(bf16[4,3,576]{2,0,1:T(4,128)(2,1)} %param.9) | copy-start | bytes 41476
  5.1 38.1 %copy-start.2 = (bf16[2048,112]{0,1:T(8,128)(2,1)S(1)}, bf16[2048,112]{0,1:T(8,128)(2,1)}, u32[]{:S(2)}) copy-start(bf16[2048,112]{0,1:T(8,128)(2,1)} %param.13) | copy-start | bytes 1376260
  5.1 61.2 %all-to-all-start = ((bf16[512,2,576]{2,1,0:T(2,128)(2,1)}), bf16[512,2,576]{2,1,0:T(2,128)(2,1)}, u32[]{:S(2)}, u32[]{:S(2)}) async-start(bf16[512,2,576]{2,1,0:T(2,128)(2,1)} %copy.15), calls=%async_computation | async-start | bytes 2621440 | tf_op jit(solution)/shard_map/all_to_all | solution.py:125
  29.2 10.3 %collective-permute-start = (bf16[48,576]{1,0:T(8,128)(2,1)S(1)}, bf16[48,576]{1,0:T(8,128)(2,1)S(1)}, u32[]{:S(2)}, u32[]{:S(2)}) collective-permute-start(bf16[48,576]{1,0:T(8,128)(2,1)S(1)} %bitcast.35), channel_id=1, source_target_pairs={{0,2},{2,4},{4,6},{6,0},{1,3},{3,5},{5,7},{7,1},{8,10},{10,12},{12... | collective-permute-start | bytes 165896 | tf_op jit(solution)/shard_map/ppermute | solution.py:133
  32.5 7.0 %collective-permute-start.2 = (bf16[48,576]{1,0:T(8,128)(2,1)S(1)}, bf16[48,576]{1,0:T(8,128)(2,1)S(1)}, u32[]{:S(2)}, u32[]{:S(2)}) collective-permute-start(bf16[48,576]{1,0:T(8,128)(2,1)S(1)} %bitcast.34), channel_id=1, source_target_pairs={{0,6},{2,0},{4,2},{6,4},{1,7},{3,1},{5,3},{7,5},{8,14},{10,8},{12,... | collective-permute-start | bytes 165896 | tf_op jit(solution)/shard_map/ppermute | solution.py:133
  35.7 7.5 %collective-permute-start.1 = (bf16[48,576]{1,0:T(8,128)(2,1)S(1)}, bf16[48,576]{1,0:T(8,128)(2,1)S(1)}, u32[]{:S(2)}, u32[]{:S(2)}) collective-permute-start(bf16[48,576]{1,0:T(8,128)(2,1)S(1)} %bitcast.33), channel_id=1, source_target_pairs={{0,4},{2,6},{4,0},{6,2},{1,5},{3,7},{5,1},{7,3},{8,12},{10,14},{12... | collective-permute-start | bytes 165896 | tf_op jit(solution)/shard_map/ppermute | solution.py:133
  43.1 39.7 %collective-permute-start.5 = (bf16[112,2048]{1,0:T(8,128)(2,1)S(1)}, bf16[112,2048]{1,0:T(8,128)(2,1)S(1)}, u32[]{:S(2)}, u32[]{:S(2)}) collective-permute-start(bf16[112,2048]{1,0:T(8,128)(2,1)S(1)} %bitcast.29), channel_id=1, source_target_pairs={{0,80},{16,64},{64,16},{80,0},{1,81},{17,65},{65,17},{81,1},{2,82}... | collective-permute-start | bytes 1376264 | tf_op jit(solution)/shard_map/ppermute | solution.py:144
  47.8 35.1 %collective-permute-start.4 = (bf16[112,2048]{1,0:T(8,128)(2,1)S(1)}, bf16[112,2048]{1,0:T(8,128)(2,1)}, u32[]{:S(2)}, u32[]{:S(2)}) collective-permute-start(bf16[112,2048]{1,0:T(8,128)(2,1)S(1)} %bitcast.30), channel_id=1, source_target_pairs={{0,64},{16,80},{64,0},{80,16},{1,65},{17,81},{65,1},{81,17},{2,66}... | collective-permute-start | bytes 1376264 | tf_op jit(solution)/shard_map/ppermute | solution.py:144
  50.0 32.8 %collective-permute-start.3 = (bf16[112,2048]{1,0:T(8,128)(2,1)S(1)}, bf16[112,2048]{1,0:T(8,128)(2,1)}, u32[]{:S(2)}, u32[]{:S(2)}) collective-permute-start(bf16[112,2048]{1,0:T(8,128)(2,1)S(1)} %bitcast.31), channel_id=1, source_target_pairs={{0,16},{16,0},{64,80},{80,64},{1,17},{17,1},{65,81},{81,65},{2,18}... | collective-permute-start | bytes 1376264 | tf_op jit(solution)/shard_map/ppermute | solution.py:144
  71.9 8.5 %all-to-all-start.1 = ((bf16[4,48,512]{2,1,0:T(8,128)(2,1)}), bf16[4,48,512]{2,1,0:T(8,128)(2,1)S(1)}, u32[]{:S(2)}, u32[]{:S(2)}) async-start(bf16[4,48,512]{2,1,0:T(8,128)(2,1)} %attend.1), calls=%async_computation.1 | async-start | bytes 393216 | tf_op jit(solution)/shard_map/all_to_all | solution.py:155
  80.4 1.6 %copy-start.1 = (bf16[16,512,128]{2,1,0:T(8,128)(2,1)S(1)}, bf16[16,512,128]{2,1,0:T(8,128)(2,1)}, u32[]{:S(2)}) copy-start(bf16[16,512,128]{2,1,0:T(8,128)(2,1)} %value_ref.1) | copy-start | bytes 6291460
  85.0 21.4 %collective-permute-start.6 = (bf16[448,2048]{1,0:T(8,128)(2,1)S(1)}, bf16[448,2048]{1,0:T(8,128)(2,1)S(1)}, u32[]{:S(2)}, u32[]{:S(2)}) collective-permute-start(bf16[448,2048]{1,0:T(8,128)(2,1)S(1)} %constant_dynamic-update-slice_fusion.own_ref), channel_id=1, source_target_pairs={{0,8},{8,0},{1,9},{9,1},{2,10},{10,2},{3,11},{11,3},{4,12},{12,4},... | collective-permute-start | bytes 5505032 | tf_op jit(solution)/shard_map/ppermute | solution.py:26

commit v5 on v4

--- a/solution.py
+++ b/solution.py
@@ -34,7 +34,7 @@
     return lax.dot_general(a, b, (((1,), (1,)), ((), ())), preferred_element_type=jnp.float32)
 
 
-def attend(steps, heads, width, place_ref, q0, q1, q2, q3, key_ref, fresh_ref, request_ref, out_ref):
+def attend(steps, heads, width, place_ref, q0, q1, q2, q3, key_ref, fresh_ref, request_ref, value_ref, out_ref):
     x, slot = place_ref[0], place_ref[2]
     lane = lax.broadcasted_iota(jnp.int32, (1, request_ref.shape[1]), 1)
     request = jnp.sum(jnp.where(lane == slot, request_ref[0:1], 0), axis=1, keepdims=True)
@@ -86,7 +86,8 @@
             out_ref[copy, :, h * vhead : (h + 1) * vhead] = value
 
 
-def project(n, place_ref, piece_ref, own_ref, other_ref, out_ref):
+def project(n, place_ref, piece_ref, *refs):
+    *weight_refs, out_ref = refs
     core, yl, zb = place_ref[1], place_ref[3], place_ref[4]
     every = piece_ref.shape[0]
     row = lax.broadcasted_iota(jnp.int32, (every, 1), 0)
@@ -98,7 +99,7 @@
     rows, depth = lines.shape[0] // 2, lines.shape[1]
     groups = out_ref.shape[0] // 8
     columns = out_ref.shape[1]
-    weight = jnp.concatenate([w[...] for w in (own_ref, other_ref)], axis=0)
+    weight = jnp.concatenate([w[...] for w in weight_refs], axis=0)
     product = dot_rows(weight[:, :depth], lines[:rows]) + dot_rows(weight[:, depth:], lines[rows:])
     for block in range(8):
         other_core, other_y, other_z = block // 4, block // 2 % 2, block % 2
@@ -146,11 +147,11 @@
     latent = pl.pallas_call(
         functools.partial(attend, steps, heads, width),
         out_shape=jax.ShapeDtypeStruct((slots, rows, width), jnp.bfloat16),
-        in_specs=[SMEM] + [VMEM] * 7,
+        in_specs=[SMEM] + [VMEM] * 8,
         out_specs=VMEM,
         compiler_params=pltpu.CompilerParams(vmem_limit_bytes=LIMIT),
         name="attend",
-    )(places, *query, keys, fresh, limits)
+    )(places, *query, keys, fresh, limits, value_weight)
 
     latent = lax.all_to_all(latent, "x", split_axis=0, concat_axis=0, tiled=True)
     count = 1
@@ -169,13 +170,13 @@
     sent = sent.reshape(count * 2 * n, heads // 2 * vhead)
     sent, *near_weights = lax.optimization_barrier((sent, *near_weights))
     piece = lax.all_to_all(sent, WIDE, split_axis=0, concat_axis=0, tiled=True)
-    weight = jnp.concatenate([weight, *near_weights], axis=0)
-    weights = (weight, swap(weight, "core"))
+    weights = [weight, *near_weights]
+    weights += [swap(part, "core") for part in weights]
     own_columns = output_weight.shape[1] // groups
     product = pl.pallas_call(
         functools.partial(project, n),
         out_shape=jax.ShapeDtypeStruct((8 * groups, own_columns, count * n), jnp.bfloat16),
-        in_specs=[SMEM] + [VMEM] * 3,
+        in_specs=[SMEM] + [VMEM] * 9,
         out_specs=VMEM,
         compiler_params=pltpu.CompilerParams(vmem_limit_bytes=LIMIT),
         name="project",

time: 131 us -> 128 us (0.977)
  blocking collectives: 38.1 us -> 31.1 us
  starting transfers between devices: 50.7 us -> 57 us
  waiting for transfers between devices: 23.2 us -> 19.3 us
    all_to_all x1, blocking collectives: 16.9 us -> 8.02 us  [on_device(): lax.all_to_all(latent, 'x', split_axis=0, concat_axis=0, tiled=True)]
    ppermute x1 -> x4, starting transfers between devices: 4.51 us -> 10.3 us  [swap(): return lax.ppermute(array, axis, [(0, 1), (1, 0)])]
    all_to_all x1, waiting for transfers between devices: 5.1 us -> 0.01 us  [on_device(): piece = lax.all_to_all(sent, WIDE, split_axis=0, concat_axis=0, tiled=True)]
    ppermute x1 -> x4, waiting for transfers between devices: 0.01 us -> 1.97 us  [swap(): return lax.ppermute(array, axis, [(0, 1), (1, 0)])]
    all_to_all x1, blocking collectives: 21.2 us -> 23.1 us  [on_device(): lax.all_to_all(product, BLOCKS + TENSOR, split_axis=0, concat_axis=0, til...]
    unnamed x18 -> x21, local copies, waits for them, and re-layouts: 4.82 us -> 4.21 us
  transfers between devices with their start and end apart: 9 -> 12, of which waited for: 3 -> 4; matrix products, arithmetic and copies ran while one was open for 3% -> 3% of each run, Pallas kernels for 2% -> 3%
where the time goes in v5:
time: 128 us; the launch traced here: 127 us
  starting transfers between devices  57 us (45%)
  blocking collectives  31.1 us (24%)
  waiting for transfers between devices  19.3 us (15%)
  local copies, waits for them, and re-layouts  12.2 us (10%)
  Pallas kernels  5.96 us (5%)
    all_to_all x1, starting transfers between devices, on_device(): lax.all_to_all(ordered, ('zh',) + DP + ('x',), split_axis=0, concat_axis=...  24 us
    all_to_all x1, blocking collectives, on_device(): lax.all_to_all(product, BLOCKS + TENSOR, split_axis=0, concat_axis=0, til...  23.1 us
    all_to_all x1, waiting for transfers between devices, on_device(): lax.all_to_all(ordered, ('zh',) + DP + ('x',), split_axis=0, concat_axis=...  14.4 us
    ppermute x3, starting transfers between devices, on_device(): both = lax.ppermute(both, 'x', [(j, (j + shift) % 4) for j in range(4)])  10.7 us
    ppermute x4, starting transfers between devices, swap(): return lax.ppermute(array, axis, [(0, 1), (1, 0)])  10.3 us
    ppermute x3, starting transfers between devices, on_device(): lax.ppermute(weight, ('yl', 'zb'), [(j, j ^ step) for j in range(4)])  8.62 us
    all_to_all x1, blocking collectives, on_device(): lax.all_to_all(latent, 'x', split_axis=0, concat_axis=0, tiled=True)  8.02 us
    unnamed x21, local copies, waits for them, and re-layouts  4.21 us
  transfers between devices with their start and end apart: 12, of which 4 were waited for; matrix products, arithmetic and copies ran while one was open for 3% of the time, Pallas kernels for 3%

profile of v5, /device:TPU:1, one launch (start us, length us, event | category | flops | bytes accessed | tf_op | source)
XLA Modules:
  0.0 127.1 jit_solution(16993727461881565315)
XLA Ops:
  0.0 0.0 copy-start
  0.0 1.1 copy-done
  1.1 1.1 convolution_convert_fusion
  2.2 0.1 pad_maximum_fusion
  2.3 2.8 %copy.15 = bf16[512,2,576]{2,1,0:T(2,128)(2,1)} copy(bf16[512,2,576]{0,2,1:T(8,128)(2,1)S(1)} %pad_maximum_fusion) | data formatting | bytes 2359296 | tf_op jit(solution)/shard_map/concatenate | solution.py:125
  5.1 0.0 copy-start.3
  5.1 24.0 %all-to-all-start = ((bf16[512,2,576]{2,1,0:T(2,128)(2,1)}), bf16[512,2,576]{2,1,0:T(2,128)(2,1)}, u32[]{:S(2)}, u32[]{:S(2)}) async-start(bf16[512,2,576]{2,1,0:T(2,128)(2,1)} %copy.15), calls=%async_computation | async-start | bytes 2621440 | tf_op jit(solution)/shard_map/all_to_all | solution.py:126
  29.1 0.0 copy-done.6
  29.2 3.3 %collective-permute-start = (bf16[48,576]{1,0:T(8,128)(2,1)S(1)}, bf16[48,576]{1,0:T(8,128)(2,1)S(1)}, u32[]{:S(2)}, u32[]{:S(2)}) collective-permute-start(bf16[48,576]{1,0:T(8,128)(2,1)S(1)} %bitcast.36), channel_id=1, source_target_pairs={{0,2},{2,4},{4,6},{6,0},{1,3},{3,5},{5,7},{7,1},{8,10},{10,12},{12... | collective-permute-start | bytes 165896 | tf_op jit(solution)/shard_map/ppermute | solution.py:134
  32.5 4.3 %collective-permute-start.1 = (bf16[48,576]{1,0:T(8,128)(2,1)S(1)}, bf16[48,576]{1,0:T(8,128)(2,1)S(1)}, u32[]{:S(2)}, u32[]{:S(2)}) collective-permute-start(bf16[48,576]{1,0:T(8,128)(2,1)S(1)} %bitcast.35), channel_id=1, source_target_pairs={{0,4},{2,6},{4,0},{6,2},{1,5},{3,7},{5,1},{7,3},{8,12},{10,14},{12... | collective-permute-start | bytes 165896 | tf_op jit(solution)/shard_map/ppermute | solution.py:134
  36.8 3.1 %collective-permute-start.2 = (bf16[48,576]{1,0:T(8,128)(2,1)S(1)}, bf16[48,576]{1,0:T(8,128)(2,1)S(1)}, u32[]{:S(2)}, u32[]{:S(2)}) collective-permute-start(bf16[48,576]{1,0:T(8,128)(2,1)S(1)} %bitcast.34), channel_id=1, source_target_pairs={{0,6},{2,0},{4,2},{6,4},{1,7},{3,1},{5,3},{7,5},{8,14},{10,8},{12,... | collective-permute-start | bytes 165896 | tf_op jit(solution)/shard_map/ppermute | solution.py:134
  39.9 0.0 copy-done.8
  39.9 0.0 copy-done.9
  40.0 0.1 stack.32.place_ref
  40.1 0.0 collective-permute-done.q1
  40.1 0.2 collective-permute-done.1.q2
  40.3 2.7 %collective-permute-done.2.q3 = bf16[48,576]{1,0:T(8,128)(2,1)S(1)} collective-permute-done((bf16[48,576]{1,0:T(8,128)(2,1)S(1)}, bf16[48,576]{1,0:T(8,128)(2,1)S(1)}, u32[]{:S(2)}, u32[]{:S(2)}) %collective-permute-start.2) | collective-permute-done | bytes 55328 | tf_op jit(solution)/shard_map/ppermute | solution.py:134
  43.0 0.0 copy-done.3
  43.0 3.3 %collective-permute-start.3 = (bf16[112,2048]{1,0:T(8,128)(2,1)S(1)}, bf16[112,2048]{1,0:T(8,128)(2,1)}, u32[]{:S(2)}, u32[]{:S(2)}) collective-permute-start(bf16[112,2048]{1,0:T(8,128)(2,1)S(1)} %bitcast.26), channel_id=1, source_target_pairs={{0,16},{16,0},{64,80},{80,64},{1,17},{17,1},{65,81},{81,65},{2,18}... | collective-permute-start | bytes 1376264 | tf_op jit(solution)/shard_map/ppermute | solution.py:145
  46.3 3.4 %collective-permute-start.4 = (bf16[112,2048]{1,0:T(8,128)(2,1)S(1)}, bf16[112,2048]{1,0:T(8,128)(2,1)}, u32[]{:S(2)}, u32[]{:S(2)}) collective-permute-start(bf16[112,2048]{1,0:T(8,128)(2,1)S(1)} %bitcast.27), channel_id=1, source_target_pairs={{0,64},{16,80},{64,0},{80,16},{1,65},{17,81},{65,1},{81,17},{2,66}... | collective-permute-start | bytes 1376264 | tf_op jit(solution)/shard_map/ppermute | solution.py:145
  49.7 1.9 %collective-permute-start.5 = (bf16[112,2048]{1,0:T(8,128)(2,1)S(1)}, bf16[112,2048]{1,0:T(8,128)(2,1)}, u32[]{:S(2)}, u32[]{:S(2)}) collective-permute-start(bf16[112,2048]{1,0:T(8,128)(2,1)S(1)} %bitcast.28), channel_id=1, source_target_pairs={{0,80},{16,64},{64,16},{80,0},{1,81},{17,65},{65,17},{81,1},{2,82}... | collective-permute-start | bytes 1376264 | tf_op jit(solution)/shard_map/ppermute | solution.py:145
  51.6 14.4 %all-to-all-done = bf16[512,2,576]{2,1,0:T(2,128)(2,1)} async-done(((bf16[512,2,576]{2,1,0:T(2,128)(2,1)}), bf16[512,2,576]{2,1,0:T(2,128)(2,1)}, u32[]{:S(2)}, u32[]{:S(2)}) %all-to-all-start) | async-done | bytes 1179680 | tf_op jit(solution)/shard_map/all_to_all | solution.py:126
  66.0 4.1 %reshape.38.key_ref = bf16[1024,576]{1,0:T(8,128)(2,1)} reshape(bf16[512,2,576]{2,1,0:T(2,128)(2,1)} %all-to-all-done) | data formatting | bytes 2359296 | tf_op jit(solution)/shard_map/reshape | solution.py:127
  70.1 1.3 %copy-done.2 = bf16[1024,576]{1,0:T(8,128)(2,1)S(1)} copy-done((bf16[1024,576]{1,0:T(8,128)(2,1)S(1)}, bf16[1024,576]{1,0:T(8,128)(2,1)}, u32[]{:S(2)}) %copy-start.2) | copy-done | bytes 1179672
  71.4 1.7 %attend.1 = bf16[4,48,512]{2,1,0:T(8,128)(2,1)S(1)} custom-call(s32[5]{0:T(128)S(1)} %stack.32.place_ref, bf16[48,576]{1,0:T(8,128)(2,1)S(1)} %bitcast.31, bf16[48,576]{1,0:T(8,128)(2,1)S(1)} %collective-permute-done.q1, bf16[48,576]{1,0:T(8,128)(2,1)S(1)} %collective-permute-done.1.q2, bf16[48,576]{1,0:T(8,128)(2,1)S(1)} %collective-permute-done.2.q3, ...), custom_call_target="tpu_custom_call" | custom-call | tf_op jit(solution)/shard_map/attend/pallas_call | solution.py:147
  73.1 8.0 %all_to_all.26.latent_ref = bf16[4,48,512]{2,1,0:T(8,128)(2,1)S(1)} all-to-all(bf16[4,48,512]{2,1,0:T(8,128)(2,1)S(1)} %attend.1), channel_id=1, replica_groups=mesh['yh'=4,'yl'=2,'za'=2,'zb'=2,'core'=2,'x'=4,'zh'=2] {'x'}, dimensions={0} | all-to-all | bytes 393216 | tf_op jit(solution)/shard_map/all_to_all | solution.py:156
  81.1 1.6 %map_values.1 = bf16[8,24,1024]{2,1,0:T(8,128)(2,1)} custom-call(bf16[4,48,512]{2,1,0:T(8,128)(2,1)S(1)} %all_to_all.26.latent_ref, bf16[16,512,128]{2,1,0:T(8,128)(2,1)S(1)} %copy-done.1), custom_call_target="tpu_custom_call" | custom-call | tf_op jit(solution)/shard_map/map_values/pallas_call | solution.py:161
  82.7 0.0 collective-permute-done.3.refs_1_
  82.7 0.0 collective-permute-done.4.refs_2_
  82.7 0.0 collective-permute-done.5.refs_3_
  82.7 3.5 %all-to-all-start.2 = ((bf16[8,24,1024]{2,1,0:T(8,128)(2,1)}), bf16[8,24,1024]{2,1,0:T(8,128)(2,1)S(1)}, u32[]{:S(2)}, u32[]{:S(2)}) async-start(bf16[8,24,1024]{2,1,0:T(8,128)(2,1)} %bitcast.14), calls=%async_computation.2 | async-start | bytes 786432 | tf_op jit(solution)/shard_map/all_to_all | solution.py:172
  86.2 4.0 %collective-permute-start.6 = (bf16[112,2048]{1,0:T(8,128)(2,1)S(1)}, bf16[112,2048]{1,0:T(8,128)(2,1)S(1)}, u32[]{:S(2)}, u32[]{:S(2)}) collective-permute-start(bf16[112,2048]{1,0:T(8,128)(2,1)S(1)} %bitcast.29), channel_id=1, source_target_pairs={{0,8},{8,0},{1,9},{9,1},{2,10},{10,2},{3,11},{11,3},{4,12},{12,4},... | collective-permute-start | bytes 1376264 | tf_op jit(solution)/shard_map/ppermute | solution.py:26
  90.2 1.9 %collective-permute-start.7 = (bf16[112,2048]{1,0:T(8,128)(2,1)}, bf16[112,2048]{1,0:T(8,128)(2,1)S(1)}, u32[]{:S(2)}, u32[]{:S(2)}) collective-permute-start(bf16[112,2048]{1,0:T(8,128)(2,1)} %collective-permute-done.3.refs_1_), channel_id=1, source_target_pairs={{0,8},{8,0},{1,9},{9,1},{2,10},{10,2},{3,11},{11,3},{4,12},{12,4},... | collective-permute-start | bytes 1376264 | tf_op jit(solution)/shard_map/ppermute | solution.py:26
  92.2 2.4 %collective-permute-start.8 = (bf16[112,2048]{1,0:T(8,128)(2,1)}, bf16[112,2048]{1,0:T(8,128)(2,1)S(1)}, u32[]{:S(2)}, u32[]{:S(2)}) collective-permute-start(bf16[112,2048]{1,0:T(8,128)(2,1)} %collective-permute-done.4.refs_2_), channel_id=1, source_target_pairs={{0,8},{8,0},{1,9},{9,1},{2,10},{10,2},{3,11},{11,3},{4,12},{12,4},... | collective-permute-start | bytes 1376264 | tf_op jit(solution)/shard_map/ppermute | solution.py:26
  94.6 1.9 %collective-permute-start.9 = (bf16[112,2048]{1,0:T(8,128)(2,1)}, bf16[112,2048]{1,0:T(8,128)(2,1)S(1)}, u32[]{:S(2)}, u32[]{:S(2)}) collective-permute-start(bf16[112,2048]{1,0:T(8,128)(2,1)} %collective-permute-done.5.refs_3_), channel_id=1, source_target_pairs={{0,8},{8,0},{1,9},{9,1},{2,10},{10,2},{3,11},{11,3},{4,12},{12,4},... | collective-permute-start | bytes 1376264 | tf_op jit(solution)/shard_map/ppermute | solution.py:26
  96.5 0.0 collective-permute-done.6.refs_4_
  96.5 0.0 collective-permute-done.7.refs_5_
  96.5 0.0 collective-permute-done.8.refs_6_
  96.5 2.0 %collective-permute-done.9.refs_7_ = bf16[112,2048]{1,0:T(8,128)(2,1)S(1)} collective-permute-done((bf16[112,2048]{1,0:T(8,128)(2,1)}, bf16[112,2048]{1,0:T(8,128)(2,1)S(1)}, u32[]{:S(2)}, u32[]{:S(2)}) %collective-permute-start.9) | collective-permute-done | bytes 458784 | tf_op jit(solution)/shard_map/ppermute | solution.py:26
  98.5 0.8 copy-done.4
  99.3 0.0 all-to-all-done.2
  99.3 1.0 copy-done.5
  100.3 2.6 %project.1 = bf16[64,14,96]{2,1,0:T(8,128)(2,1)S(1)} custom-call(s32[5]{0:T(128)S(1)} %stack.32.place_ref, bf16[192,1024]{1,0:T(8,128)(2,1)S(1)} %bitcast.25, bf16[112,2048]{1,0:T(8,128)(2,1)S(1)} %bitcast.30, bf16[112,2048]{1,0:T(8,128)(2,1)} %collective-permute-done.3.refs_1_, bf16[112,2048]{1,0:T(8,128)(2,1)} %collective-permute-done.4.refs_2_, ...), custom_call_target="tpu_custom_call" | custom-call | tf_op jit(solution)/shard_map/project/pallas_call | solution.py:176
  102.9 23.1 %all_to_all.27 = bf16[64,14,96]{2,1,0:T(8,128)(2,1)S(1)} all-to-all(bf16[64,14,96]{2,1,0:T(8,128)(2,1)S(1)} %project.1), channel_id=1, replica_groups=mesh['yh'=4,'yl'=2,'za'=2,'zb'=2,'core'=2,'x'=4,'zh'=2] {'yl','zb','core..., dimensions={0} | all-to-all | bytes 344064 | tf_op jit(solution)/shard_map/all_to_all | solution.py:184
  126.1 0.1 bitcast_reduce_fusion
  126.1 0.2 copy.16
  126.3 0.1 copy.17
  126.4 0.7 copy.18
  (14 shorter events, 0.1 us)
Async XLA Ops:
  0.0 1.1 copy-start
  5.1 24.0 %copy-start.6 = (bf16[4,3,16,576]{3,2,1,0:T(8,128)(2,1)S(1)}, bf16[4,3,16,576]{3,2,1,0:T(8,128)(2,1)}, u32[]{:S(2)}) copy-start(bf16[4,3,16,576]{3,2,1,0:T(8,128)(2,1)} %param.8) | copy-start | bytes 663556
  5.1 34.8 %copy-start.8 = (s32[256]{0:T(256)S(1)}, s32[256]{0:T(256)}, u32[]{:S(2)}) copy-start(s32[256]{0:T(256)} %param.11) | copy-start | bytes 3076
  5.1 34.8 %copy-start.9 = (s32[256]{0:T(256)S(1)}, s32[256]{0:T(256)}, u32[]{:S(2)}) copy-start(s32[256]{0:T(256)} %param.10) | copy-start | bytes 3076
  5.1 34.8 %copy-start.7 = (bf16[4,3,576]{2,0,1:T(4,128)(2,1)S(1)}, bf16[4,3,576]{2,0,1:T(4,128)(2,1)}, u32[]{:S(2)}) copy-start(bf16[4,3,576]{2,0,1:T(4,128)(2,1)} %param.9) | copy-start | bytes 41476
  5.1 37.9 %copy-start.3 = (bf16[2048,112]{0,1:T(8,128)(2,1)S(1)}, bf16[2048,112]{0,1:T(8,128)(2,1)}, u32[]{:S(2)}) copy-start(bf16[2048,112]{0,1:T(8,128)(2,1)} %param.13) | copy-start | bytes 1376260
  5.1 60.9 %all-to-all-start = ((bf16[512,2,576]{2,1,0:T(2,128)(2,1)}), bf16[512,2,576]{2,1,0:T(2,128)(2,1)}, u32[]{:S(2)}, u32[]{:S(2)}) async-start(bf16[512,2,576]{2,1,0:T(2,128)(2,1)} %copy.15), calls=%async_computation | async-start | bytes 2621440 | tf_op jit(solution)/shard_map/all_to_all | solution.py:126
  29.2 10.9 %collective-permute-start = (bf16[48,576]{1,0:T(8,128)(2,1)S(1)}, bf16[48,576]{1,0:T(8,128)(2,1)S(1)}, u32[]{:S(2)}, u32[]{:S(2)}) collective-permute-start(bf16[48,576]{1,0:T(8,128)(2,1)S(1)} %bitcast.36), channel_id=1, source_target_pairs={{0,2},{2,4},{4,6},{6,0},{1,3},{3,5},{5,7},{7,1},{8,10},{10,12},{12... | collective-permute-start | bytes 165896 | tf_op jit(solution)/shard_map/ppermute | solution.py:134
  32.5 7.8 %collective-permute-start.1 = (bf16[48,576]{1,0:T(8,128)(2,1)S(1)}, bf16[48,576]{1,0:T(8,128)(2,1)S(1)}, u32[]{:S(2)}, u32[]{:S(2)}) collective-permute-start(bf16[48,576]{1,0:T(8,128)(2,1)S(1)} %bitcast.35), channel_id=1, source_target_pairs={{0,4},{2,6},{4,0},{6,2},{1,5},{3,7},{5,1},{7,3},{8,12},{10,14},{12... | collective-permute-start | bytes 165896 | tf_op jit(solution)/shard_map/ppermute | solution.py:134
  36.8 6.2 %collective-permute-start.2 = (bf16[48,576]{1,0:T(8,128)(2,1)S(1)}, bf16[48,576]{1,0:T(8,128)(2,1)S(1)}, u32[]{:S(2)}, u32[]{:S(2)}) collective-permute-start(bf16[48,576]{1,0:T(8,128)(2,1)S(1)} %bitcast.34), channel_id=1, source_target_pairs={{0,6},{2,0},{4,2},{6,4},{1,7},{3,1},{5,3},{7,5},{8,14},{10,8},{12,... | collective-permute-start | bytes 165896 | tf_op jit(solution)/shard_map/ppermute | solution.py:134
  43.0 27.1 %copy-start.1 = (bf16[16,512,128]{2,1,0:T(8,128)(2,1)S(1)}, bf16[16,512,128]{2,1,0:T(8,128)(2,1)}, u32[]{:S(2)}) copy-start(bf16[16,512,128]{2,1,0:T(8,128)(2,1)} %value_ref.3) | copy-start | bytes 6291460
  43.0 39.7 %collective-permute-start.3 = (bf16[112,2048]{1,0:T(8,128)(2,1)S(1)}, bf16[112,2048]{1,0:T(8,128)(2,1)}, u32[]{:S(2)}, u32[]{:S(2)}) collective-permute-start(bf16[112,2048]{1,0:T(8,128)(2,1)S(1)} %bitcast.26), channel_id=1, source_target_pairs={{0,16},{16,0},{64,80},{80,64},{1,17},{17,1},{65,81},{81,65},{2,18}... | collective-permute-start | bytes 1376264 | tf_op jit(solution)/shard_map/ppermute | solution.py:145
  46.3 36.4 %collective-permute-start.4 = (bf16[112,2048]{1,0:T(8,128)(2,1)S(1)}, bf16[112,2048]{1,0:T(8,128)(2,1)}, u32[]{:S(2)}, u32[]{:S(2)}) collective-permute-start(bf16[112,2048]{1,0:T(8,128)(2,1)S(1)} %bitcast.27), channel_id=1, source_target_pairs={{0,64},{16,80},{64,0},{80,16},{1,65},{17,81},{65,1},{81,17},{2,66}... | collective-permute-start | bytes 1376264 | tf_op jit(solution)/shard_map/ppermute | solution.py:145
  49.7 33.0 %collective-permute-start.5 = (bf16[112,2048]{1,0:T(8,128)(2,1)S(1)}, bf16[112,2048]{1,0:T(8,128)(2,1)}, u32[]{:S(2)}, u32[]{:S(2)}) collective-permute-start(bf16[112,2048]{1,0:T(8,128)(2,1)S(1)} %bitcast.28), channel_id=1, source_target_pairs={{0,80},{16,64},{64,16},{80,0},{1,81},{17,65},{65,17},{81,1},{2,82}... | collective-permute-start | bytes 1376264 | tf_op jit(solution)/shard_map/ppermute | solution.py:145
  70.1 1.3 %copy-start.2 = (bf16[1024,576]{1,0:T(8,128)(2,1)S(1)}, bf16[1024,576]{1,0:T(8,128)(2,1)}, u32[]{:S(2)}) copy-start(bf16[1024,576]{1,0:T(8,128)(2,1)} %reshape.38.key_ref) | copy-start | bytes 3538948
  82.7 16.5 %all-to-all-start.2 = ((bf16[8,24,1024]{2,1,0:T(8,128)(2,1)}), bf16[8,24,1024]{2,1,0:T(8,128)(2,1)S(1)}, u32[]{:S(2)}, u32[]{:S(2)}) async-start(bf16[8,24,1024]{2,1,0:T(8,128)(2,1)} %bitcast.14), calls=%async_computation.2 | async-start | bytes 786432 | tf_op jit(solution)/shard_map/all_to_all | solution.py:172
  86.2 10.3 %collective-permute-start.6 = (bf16[112,2048]{1,0:T(8,128)(2,1)S(1)}, bf16[112,2048]{1,0:T(8,128)(2,1)S(1)}, u32[]{:S(2)}, u32[]{:S(2)}) collective-permute-start(bf16[112,2048]{1,0:T(8,128)(2,1)S(1)} %bitcast.29), channel_id=1, source_target_pairs={{0,8},{8,0},{1,9},{9,1},{2,10},{10,2},{3,11},{11,3},{4,12},{12,4},... | collective-permute-start | bytes 1376264 | tf_op jit(solution)/shard_map/ppermute | solution.py:26
  90.2 6.3 %collective-permute-start.7 = (bf16[112,2048]{1,0:T(8,128)(2,1)}, bf16[112,2048]{1,0:T(8,128)(2,1)S(1)}, u32[]{:S(2)}, u32[]{:S(2)}) collective-permute-start(bf16[112,2048]{1,0:T(8,128)(2,1)} %collective-permute-done.3.refs_1_), channel_id=1, source_target_pairs={{0,8},{8,0},{1,9},{9,1},{2,10},{10,2},{3,11},{11,3},{4,12},{12,4},... | collective-permute-start | bytes 1376264 | tf_op jit(solution)/shard_map/ppermute | solution.py:26
  92.2 4.4 %collective-permute-start.8 = (bf16[112,2048]{1,0:T(8,128)(2,1)}, bf16[112,2048]{1,0:T(8,128)(2,1)S(1)}, u32[]{:S(2)}, u32[]{:S(2)}) collective-permute-start(bf16[112,2048]{1,0:T(8,128)(2,1)} %collective-permute-done.4.refs_2_), channel_id=1, source_target_pairs={{0,8},{8,0},{1,9},{9,1},{2,10},{10,2},{3,11},{11,3},{4,12},{12,4},... | collective-permute-start | bytes 1376264 | tf_op jit(solution)/shard_map/ppermute | solution.py:26
  94.6 3.9 %collective-permute-start.9 = (bf16[112,2048]{1,0:T(8,128)(2,1)}, bf16[112,2048]{1,0:T(8,128)(2,1)S(1)}, u32[]{:S(2)}, u32[]{:S(2)}) collective-permute-start(bf16[112,2048]{1,0:T(8,128)(2,1)} %collective-permute-done.5.refs_3_), channel_id=1, source_target_pairs={{0,8},{8,0},{1,9},{9,1},{2,10},{10,2},{3,11},{11,3},{4,12},{12,4},... | collective-permute-start | bytes 1376264 | tf_op jit(solution)/shard_map/ppermute | solution.py:26
  98.5 0.8 copy-start.4
  99.3 1.0 copy-start.5

commit v6 on v5

--- a/solution.py
+++ b/solution.py
@@ -34,7 +34,7 @@
     return lax.dot_general(a, b, (((1,), (1,)), ((), ())), preferred_element_type=jnp.float32)
 
 
-def attend(steps, heads, width, place_ref, q0, q1, q2, q3, key_ref, fresh_ref, request_ref, value_ref, out_ref):
+def attend(steps, heads, width, place_ref, q0, q1, q2, q3, key_ref, fresh_ref, request_ref, value_ref, weight_ref, out_ref):
     x, slot = place_ref[0], place_ref[2]
     lane = lax.broadcasted_iota(jnp.int32, (1, request_ref.shape[1]), 1)
     request = jnp.sum(jnp.where(lane == slot, request_ref[0:1], 0), axis=1, keepdims=True)
@@ -141,17 +141,18 @@
     weight, places, limits, fresh, *query = lax.optimization_barrier(
         (output_weight.T, places, limits, fresh, *query)
     )
+    other_weight = swap(weight, "core")
     near_weights = [
         lax.ppermute(weight, ("yl", "zb"), [(j, j ^ step) for j in range(4)]) for step in (1, 2, 3)
     ]
     latent = pl.pallas_call(
         functools.partial(attend, steps, heads, width),
         out_shape=jax.ShapeDtypeStruct((slots, rows, width), jnp.bfloat16),
-        in_specs=[SMEM] + [VMEM] * 8,
+        in_specs=[SMEM] + [VMEM] * 9,
         out_specs=VMEM,
         compiler_params=pltpu.CompilerParams(vmem_limit_bytes=LIMIT),
         name="attend",
-    )(places, *query, keys, fresh, limits, value_weight)
+    )(places, *query, keys, fresh, limits, value_weight, other_weight)
 
     latent = lax.all_to_all(latent, "x", split_axis=0, concat_axis=0, tiled=True)
     count = 1
@@ -170,8 +171,7 @@
     sent = sent.reshape(count * 2 * n, heads // 2 * vhead)
     sent, *near_weights = lax.optimization_barrier((sent, *near_weights))
     piece = lax.all_to_all(sent, WIDE, split_axis=0, concat_axis=0, tiled=True)
-    weights = [weight, *near_weights]
-    weights += [swap(part, "core") for part in weights]
+    weights = [weight, *near_weights, other_weight] + [swap(part, "core") for part in near_weights]
     own_columns = output_weight.shape[1] // groups
     product = pl.pallas_call(
         functools.partial(project, n),

time: 128 us -> 128 us (level)
  waiting for transfers between devices: 19.3 us -> 13.4 us
  blocking collectives: 31.1 us -> 34.8 us
  starting transfers between devices: 57 us -> 60 us
    all_to_all x1, waiting for transfers between devices: 14.4 us -> 8.78 us  [on_device(): lax.all_to_all(ordered, ('zh',) + DP + ('x',), split_axis=0, concat_axis=...]
    ppermute x4, starting transfers between devices: 10.3 us -> 13.5 us  [swap(): return lax.ppermute(array, axis, [(0, 1), (1, 0)])]
    all_to_all x1, blocking collectives: 23.1 us -> 26.1 us  [on_device(): lax.all_to_all(product, BLOCKS + TENSOR, split_axis=0, concat_axis=0, til...]
    unnamed x21 -> x17, local copies, waits for them, and re-layouts: 4.21 us -> 3.42 us
  transfers between devices with their start and end apart: 12 -> 12, of which waited for: 4 -> 5; matrix products, arithmetic and copies ran while one was open for 3% -> 3% of each run, Pallas kernels for 3% -> 3%
where the time goes in v6:
time: 128 us; the launch traced here: 127 us
  starting transfers between devices  60 us (47%)
  blocking collectives  34.8 us (27%)
  waiting for transfers between devices  13.4 us (10%)
  local copies, waits for them, and re-layouts  11.4 us (9%)
  Pallas kernels  5.94 us (5%)
    all_to_all x1, blocking collectives, on_device(): lax.all_to_all(product, BLOCKS + TENSOR, split_axis=0, concat_axis=0, til...  26.1 us
    all_to_all x1, starting transfers between devices, on_device(): lax.all_to_all(ordered, ('zh',) + DP + ('x',), split_axis=0, concat_axis=...  24 us
    ppermute x4, starting transfers between devices, swap(): return lax.ppermute(array, axis, [(0, 1), (1, 0)])  13.5 us
    ppermute x3, starting transfers between devices, on_device(): both = lax.ppermute(both, 'x', [(j, (j + shift) % 4) for j in range(4)])  10.7 us
    all_to_all x1, waiting for transfers between devices, on_device(): lax.all_to_all(ordered, ('zh',) + DP + ('x',), split_axis=0, concat_axis=...  8.78 us
    all_to_all x1, blocking collectives, on_device(): lax.all_to_all(latent, 'x', split_axis=0, concat_axis=0, tiled=True)  8.65 us
    ppermute x3, starting transfers between devices, on_device(): lax.ppermute(weight, ('yl', 'zb'), [(j, j ^ step) for j in range(4)])  8.38 us
    reshape x1, local copies, waits for them, and re-layouts, on_device(): keys = keys.reshape(-1, depth)  4.06 us
  transfers between devices with their start and end apart: 12, of which 5 were waited for; matrix products, arithmetic and copies ran while one was open for 3% of the time, Pallas kernels for 3%

profile of v6, /device:TPU:1, one launch (start us, length us, event | category | flops | bytes accessed | tf_op | source)
XLA Modules:
  0.0 127.1 jit_solution(7776463713756897229)
XLA Ops:
  0.0 0.0 copy-start
  0.0 1.1 copy-done
  1.1 1.1 convolution_convert_fusion
  2.2 0.1 pad_maximum_fusion
  2.3 2.8 %copy.15 = bf16[512,2,576]{2,1,0:T(2,128)(2,1)} copy(bf16[512,2,576]{0,2,1:T(8,128)(2,1)S(1)} %pad_maximum_fusion) | data formatting | bytes 2359296 | tf_op jit(solution)/shard_map/concatenate | solution.py:125
  5.1 0.0 copy-start.4
  5.1 24.0 %all-to-all-start = ((bf16[512,2,576]{2,1,0:T(2,128)(2,1)}), bf16[512,2,576]{2,1,0:T(2,128)(2,1)}, u32[]{:S(2)}, u32[]{:S(2)}) async-start(bf16[512,2,576]{2,1,0:T(2,128)(2,1)} %copy.15), calls=%async_computation | async-start | bytes 2621440 | tf_op jit(solution)/shard_map/all_to_all | solution.py:126
  29.1 0.0 copy-done.4
  29.1 3.3 %collective-permute-start = (bf16[48,576]{1,0:T(8,128)(2,1)S(1)}, bf16[48,576]{1,0:T(8,128)(2,1)S(1)}, u32[]{:S(2)}, u32[]{:S(2)}) collective-permute-start(bf16[48,576]{1,0:T(8,128)(2,1)S(1)} %bitcast.36), channel_id=1, source_target_pairs={{0,2},{2,4},{4,6},{6,0},{1,3},{3,5},{5,7},{7,1},{8,10},{10,12},{12... | collective-permute-start | bytes 165896 | tf_op jit(solution)/shard_map/ppermute | solution.py:134
  32.4 4.3 %collective-permute-start.1 = (bf16[48,576]{1,0:T(8,128)(2,1)S(1)}, bf16[48,576]{1,0:T(8,128)(2,1)S(1)}, u32[]{:S(2)}, u32[]{:S(2)}) collective-permute-start(bf16[48,576]{1,0:T(8,128)(2,1)S(1)} %bitcast.35), channel_id=1, source_target_pairs={{0,4},{2,6},{4,0},{6,2},{1,5},{3,7},{5,1},{7,3},{8,12},{10,14},{12... | collective-permute-start | bytes 165896 | tf_op jit(solution)/shard_map/ppermute | solution.py:134
  36.8 3.1 %collective-permute-start.2 = (bf16[48,576]{1,0:T(8,128)(2,1)S(1)}, bf16[48,576]{1,0:T(8,128)(2,1)S(1)}, u32[]{:S(2)}, u32[]{:S(2)}) collective-permute-start(bf16[48,576]{1,0:T(8,128)(2,1)S(1)} %bitcast.34), channel_id=1, source_target_pairs={{0,6},{2,0},{4,2},{6,4},{1,7},{3,1},{5,3},{7,5},{8,14},{10,8},{12,... | collective-permute-start | bytes 165896 | tf_op jit(solution)/shard_map/ppermute | solution.py:134
  39.9 0.0 copy-done.6
  39.9 0.0 copy-done.7
  39.9 0.0 copy-done.5
  40.0 0.1 stack.32.place_ref
  40.0 0.0 collective-permute-done.q1
  40.0 0.2 collective-permute-done.1.q2
  40.3 2.8 %collective-permute-done.2.q3 = bf16[48,576]{1,0:T(8,128)(2,1)S(1)} collective-permute-done((bf16[48,576]{1,0:T(8,128)(2,1)S(1)}, bf16[48,576]{1,0:T(8,128)(2,1)S(1)}, u32[]{:S(2)}, u32[]{:S(2)}) %collective-permute-start.2) | collective-permute-done | bytes 55328 | tf_op jit(solution)/shard_map/ppermute | solution.py:134
  43.0 5.1 %collective-permute-start.3 = (bf16[112,2048]{1,0:T(8,128)(2,1)}, bf16[112,2048]{1,0:T(8,128)(2,1)S(1)}, u32[]{:S(2)}, u32[]{:S(2)}) collective-permute-start(bf16[112,2048]{1,0:T(8,128)(2,1)} %bitcast.26), channel_id=1, source_target_pairs={{0,8},{8,0},{1,9},{9,1},{2,10},{10,2},{3,11},{11,3},{4,12},{12,4},... | collective-permute-start | bytes 1376264 | tf_op jit(solution)/shard_map/ppermute | solution.py:26
  48.2 1.9 %collective-permute-start.4 = (bf16[112,2048]{1,0:T(8,128)(2,1)}, bf16[112,2048]{1,0:T(8,128)(2,1)}, u32[]{:S(2)}, u32[]{:S(2)}) collective-permute-start(bf16[112,2048]{1,0:T(8,128)(2,1)} %bitcast.27), channel_id=1, source_target_pairs={{0,16},{16,0},{64,80},{80,64},{1,17},{17,1},{65,81},{81,65},{2,18}... | collective-permute-start | bytes 1376264 | tf_op jit(solution)/shard_map/ppermute | solution.py:146
  50.1 2.8 %collective-permute-start.5 = (bf16[112,2048]{1,0:T(8,128)(2,1)}, bf16[112,2048]{1,0:T(8,128)(2,1)}, u32[]{:S(2)}, u32[]{:S(2)}) collective-permute-start(bf16[112,2048]{1,0:T(8,128)(2,1)} %bitcast.28), channel_id=1, source_target_pairs={{0,64},{16,80},{64,0},{80,16},{1,65},{17,81},{65,1},{81,17},{2,66}... | collective-permute-start | bytes 1376264 | tf_op jit(solution)/shard_map/ppermute | solution.py:146
  52.9 3.6 %collective-permute-start.6 = (bf16[112,2048]{1,0:T(8,128)(2,1)}, bf16[112,2048]{1,0:T(8,128)(2,1)}, u32[]{:S(2)}, u32[]{:S(2)}) collective-permute-start(bf16[112,2048]{1,0:T(8,128)(2,1)} %bitcast.29), channel_id=1, source_target_pairs={{0,80},{16,64},{64,16},{80,0},{1,81},{17,65},{65,17},{81,1},{2,82}... | collective-permute-start | bytes 1376264 | tf_op jit(solution)/shard_map/ppermute | solution.py:146
  56.6 8.8 %all-to-all-done = bf16[512,2,576]{2,1,0:T(2,128)(2,1)} async-done(((bf16[512,2,576]{2,1,0:T(2,128)(2,1)}), bf16[512,2,576]{2,1,0:T(2,128)(2,1)}, u32[]{:S(2)}, u32[]{:S(2)}) %all-to-all-start) | async-done | bytes 1179680 | tf_op jit(solution)/shard_map/all_to_all | solution.py:126
  65.4 4.1 %reshape.38.key_ref = bf16[1024,576]{1,0:T(8,128)(2,1)} reshape(bf16[512,2,576]{2,1,0:T(2,128)(2,1)} %all-to-all-done) | data formatting | bytes 2359296 | tf_op jit(solution)/shard_map/reshape | solution.py:127
  69.4 0.0 collective-permute-done.3.weight_ref.refs_4_
  69.4 0.0 copy-done.1
  69.4 1.3 %copy-done.2 = bf16[1024,576]{1,0:T(8,128)(2,1)S(1)} copy-done((bf16[1024,576]{1,0:T(8,128)(2,1)S(1)}, bf16[1024,576]{1,0:T(8,128)(2,1)}, u32[]{:S(2)}) %copy-start.2) | copy-done | bytes 1179672
  70.7 1.7 %attend.1 = bf16[4,48,512]{2,1,0:T(8,128)(2,1)S(1)} custom-call(s32[5]{0:T(128)S(1)} %stack.32.place_ref, bf16[48,576]{1,0:T(8,128)(2,1)S(1)} %bitcast.31, bf16[48,576]{1,0:T(8,128)(2,1)S(1)} %collective-permute-done.q1, bf16[48,576]{1,0:T(8,128)(2,1)S(1)} %collective-permute-done.1.q2, bf16[48,576]{1,0:T(8,128)(2,1)S(1)} %collective-permute-done.2.q3, ...), custom_call_target="tpu_custom_call" | custom-call | tf_op jit(solution)/shard_map/attend/pallas_call | solution.py:148
  72.4 8.7 %all_to_all.26.latent_ref = bf16[4,48,512]{2,1,0:T(8,128)(2,1)S(1)} all-to-all(bf16[4,48,512]{2,1,0:T(8,128)(2,1)S(1)} %attend.1), channel_id=1, replica_groups=mesh['yh'=4,'yl'=2,'za'=2,'zb'=2,'core'=2,'x'=4,'zh'=2] {'x'}, dimensions={0} | all-to-all | bytes 393216 | tf_op jit(solution)/shard_map/all_to_all | solution.py:157
  81.1 1.6 %map_values.1 = bf16[8,24,1024]{2,1,0:T(8,128)(2,1)} custom-call(bf16[4,48,512]{2,1,0:T(8,128)(2,1)S(1)} %all_to_all.26.latent_ref, bf16[16,512,128]{2,1,0:T(8,128)(2,1)S(1)} %copy-done.1), custom_call_target="tpu_custom_call" | custom-call | tf_op jit(solution)/shard_map/map_values/pallas_call | solution.py:162
  82.7 0.0 collective-permute-done.4.refs_1_
  82.7 0.0 collective-permute-done.5.refs_2_
  82.7 0.0 collective-permute-done.6.refs_3_
  82.7 3.5 %all-to-all-start.2 = ((bf16[8,24,1024]{2,1,0:T(8,128)(2,1)}), bf16[8,24,1024]{2,1,0:T(8,128)(2,1)S(1)}, u32[]{:S(2)}, u32[]{:S(2)}) async-start(bf16[8,24,1024]{2,1,0:T(8,128)(2,1)} %bitcast.14), calls=%async_computation.2 | async-start | bytes 786432 | tf_op jit(solution)/shard_map/all_to_all | solution.py:173
  86.2 4.0 %collective-permute-start.7 = (bf16[112,2048]{1,0:T(8,128)(2,1)}, bf16[112,2048]{1,0:T(8,128)(2,1)S(1)}, u32[]{:S(2)}, u32[]{:S(2)}) collective-permute-start(bf16[112,2048]{1,0:T(8,128)(2,1)} %collective-permute-done.4.refs_1_), channel_id=1, source_target_pairs={{0,8},{8,0},{1,9},{9,1},{2,10},{10,2},{3,11},{11,3},{4,12},{12,4},... | collective-permute-start | bytes 1376264 | tf_op jit(solution)/shard_map/ppermute | solution.py:26
  90.2 1.9 %collective-permute-start.8 = (bf16[112,2048]{1,0:T(8,128)(2,1)}, bf16[112,2048]{1,0:T(8,128)(2,1)S(1)}, u32[]{:S(2)}, u32[]{:S(2)}) collective-permute-start(bf16[112,2048]{1,0:T(8,128)(2,1)} %collective-permute-done.5.refs_2_), channel_id=1, source_target_pairs={{0,8},{8,0},{1,9},{9,1},{2,10},{10,2},{3,11},{11,3},{4,12},{12,4},... | collective-permute-start | bytes 1376264 | tf_op jit(solution)/shard_map/ppermute | solution.py:26
  92.1 2.4 %collective-permute-start.9 = (bf16[112,2048]{1,0:T(8,128)(2,1)}, bf16[112,2048]{1,0:T(8,128)(2,1)S(1)}, u32[]{:S(2)}, u32[]{:S(2)}) collective-permute-start(bf16[112,2048]{1,0:T(8,128)(2,1)} %collective-permute-done.6.refs_3_), channel_id=1, source_target_pairs={{0,8},{8,0},{1,9},{9,1},{2,10},{10,2},{3,11},{11,3},{4,12},{12,4},... | collective-permute-start | bytes 1376264 | tf_op jit(solution)/shard_map/ppermute | solution.py:26
  94.6 0.0 collective-permute-done.7.refs_5_
  94.6 0.0 collective-permute-done.8.refs_6_
  94.6 1.6 %collective-permute-done.9.refs_7_ = bf16[112,2048]{1,0:T(8,128)(2,1)S(1)} collective-permute-done((bf16[112,2048]{1,0:T(8,128)(2,1)}, bf16[112,2048]{1,0:T(8,128)(2,1)S(1)}, u32[]{:S(2)}, u32[]{:S(2)}) %collective-permute-start.9) | collective-permute-done | bytes 458784 | tf_op jit(solution)/shard_map/ppermute | solution.py:26
  96.2 0.1 all-to-all-done.2
  96.2 1.0 copy-done.3
  97.3 2.6 %project.1 = bf16[64,14,96]{2,1,0:T(8,128)(2,1)S(1)} custom-call(s32[5]{0:T(128)S(1)} %stack.32.place_ref, bf16[192,1024]{1,0:T(8,128)(2,1)S(1)} %bitcast.25, bf16[112,2048]{1,0:T(8,128)(2,1)S(1)} %bitcast.30, bf16[112,2048]{1,0:T(8,128)(2,1)} %collective-permute-done.4.refs_1_, bf16[112,2048]{1,0:T(8,128)(2,1)} %collective-permute-done.5.refs_2_, ...), custom_call_target="tpu_custom_call" | custom-call | tf_op jit(solution)/shard_map/project/pallas_call | solution.py:176
  99.9 26.1 %all_to_all.27 = bf16[64,14,96]{2,1,0:T(8,128)(2,1)S(1)} all-to-all(bf16[64,14,96]{2,1,0:T(8,128)(2,1)S(1)} %project.1), channel_id=1, replica_groups=mesh['yh'=4,'yl'=2,'za'=2,'zb'=2,'core'=2,'x'=4,'zh'=2] {'yl','zb','core..., dimensions={0} | all-to-all | bytes 344064 | tf_op jit(solution)/shard_map/all_to_all | solution.py:184
  126.0 0.1 bitcast_reduce_fusion
  126.1 0.2 copy.16
  126.3 0.1 copy.17
  126.4 0.7 copy.18
  (10 shorter events, 0.1 us)
Async XLA Ops:
  0.0 1.1 copy-start
  5.1 24.0 %copy-start.4 = (bf16[4,3,16,576]{3,2,1,0:T(8,128)(2,1)S(1)}, bf16[4,3,16,576]{3,2,1,0:T(8,128)(2,1)}, u32[]{:S(2)}) copy-start(bf16[4,3,16,576]{3,2,1,0:T(8,128)(2,1)} %param.8) | copy-start | bytes 663556
  5.1 34.8 %copy-start.6 = (s32[256]{0:T(256)S(1)}, s32[256]{0:T(256)}, u32[]{:S(2)}) copy-start(s32[256]{0:T(256)} %param.11) | copy-start | bytes 3076
  5.1 34.8 %copy-start.7 = (s32[256]{0:T(256)S(1)}, s32[256]{0:T(256)}, u32[]{:S(2)}) copy-start(s32[256]{0:T(256)} %param.10) | copy-start | bytes 3076
  5.1 34.8 %copy-start.5 = (bf16[4,3,576]{2,0,1:T(4,128)(2,1)S(1)}, bf16[4,3,576]{2,0,1:T(4,128)(2,1)}, u32[]{:S(2)}) copy-start(bf16[4,3,576]{2,0,1:T(4,128)(2,1)} %param.9) | copy-start | bytes 41476
  5.1 60.3 %all-to-all-start = ((bf16[512,2,576]{2,1,0:T(2,128)(2,1)}), bf16[512,2,576]{2,1,0:T(2,128)(2,1)}, u32[]{:S(2)}, u32[]{:S(2)}) async-start(bf16[512,2,576]{2,1,0:T(2,128)(2,1)} %copy.15), calls=%async_computation | async-start | bytes 2621440 | tf_op jit(solution)/shard_map/all_to_all | solution.py:126
  29.1 10.9 %collective-permute-start = (bf16[48,576]{1,0:T(8,128)(2,1)S(1)}, bf16[48,576]{1,0:T(8,128)(2,1)S(1)}, u32[]{:S(2)}, u32[]{:S(2)}) collective-permute-start(bf16[48,576]{1,0:T(8,128)(2,1)S(1)} %bitcast.36), channel_id=1, source_target_pairs={{0,2},{2,4},{4,6},{6,0},{1,3},{3,5},{5,7},{7,1},{8,10},{10,12},{12... | collective-permute-start | bytes 165896 | tf_op jit(solution)/shard_map/ppermute | solution.py:134
  32.4 7.8 %collective-permute-start.1 = (bf16[48,576]{1,0:T(8,128)(2,1)S(1)}, bf16[48,576]{1,0:T(8,128)(2,1)S(1)}, u32[]{:S(2)}, u32[]{:S(2)}) collective-permute-start(bf16[48,576]{1,0:T(8,128)(2,1)S(1)} %bitcast.35), channel_id=1, source_target_pairs={{0,4},{2,6},{4,0},{6,2},{1,5},{3,7},{5,1},{7,3},{8,12},{10,14},{12... | collective-permute-start | bytes 165896 | tf_op jit(solution)/shard_map/ppermute | solution.py:134
  36.8 6.3 %collective-permute-start.2 = (bf16[48,576]{1,0:T(8,128)(2,1)S(1)}, bf16[48,576]{1,0:T(8,128)(2,1)S(1)}, u32[]{:S(2)}, u32[]{:S(2)}) collective-permute-start(bf16[48,576]{1,0:T(8,128)(2,1)S(1)} %bitcast.34), channel_id=1, source_target_pairs={{0,6},{2,0},{4,2},{6,4},{1,7},{3,1},{5,3},{7,5},{8,14},{10,8},{12,... | collective-permute-start | bytes 165896 | tf_op jit(solution)/shard_map/ppermute | solution.py:134
  43.0 26.4 %copy-start.1 = (bf16[16,512,128]{2,1,0:T(8,128)(2,1)S(1)}, bf16[16,512,128]{2,1,0:T(8,128)(2,1)}, u32[]{:S(2)}) copy-start(bf16[16,512,128]{2,1,0:T(8,128)(2,1)} %value_ref.3) | copy-start | bytes 6291460
  43.0 26.4 %collective-permute-start.3 = (bf16[112,2048]{1,0:T(8,128)(2,1)}, bf16[112,2048]{1,0:T(8,128)(2,1)S(1)}, u32[]{:S(2)}, u32[]{:S(2)}) collective-permute-start(bf16[112,2048]{1,0:T(8,128)(2,1)} %bitcast.26), channel_id=1, source_target_pairs={{0,8},{8,0},{1,9},{9,1},{2,10},{10,2},{3,11},{11,3},{4,12},{12,4},... | collective-permute-start | bytes 1376264 | tf_op jit(solution)/shard_map/ppermute | solution.py:26
  48.2 34.5 %collective-permute-start.4 = (bf16[112,2048]{1,0:T(8,128)(2,1)}, bf16[112,2048]{1,0:T(8,128)(2,1)}, u32[]{:S(2)}, u32[]{:S(2)}) collective-permute-start(bf16[112,2048]{1,0:T(8,128)(2,1)} %bitcast.27), channel_id=1, source_target_pairs={{0,16},{16,0},{64,80},{80,64},{1,17},{17,1},{65,81},{81,65},{2,18}... | collective-permute-start | bytes 1376264 | tf_op jit(solution)/shard_map/ppermute | solution.py:146
  50.1 32.6 %collective-permute-start.5 = (bf16[112,2048]{1,0:T(8,128)(2,1)}, bf16[112,2048]{1,0:T(8,128)(2,1)}, u32[]{:S(2)}, u32[]{:S(2)}) collective-permute-start(bf16[112,2048]{1,0:T(8,128)(2,1)} %bitcast.28), channel_id=1, source_target_pairs={{0,64},{16,80},{64,0},{80,16},{1,65},{17,81},{65,1},{81,17},{2,66}... | collective-permute-start | bytes 1376264 | tf_op jit(solution)/shard_map/ppermute | solution.py:146
  52.9 29.8 %collective-permute-start.6 = (bf16[112,2048]{1,0:T(8,128)(2,1)}, bf16[112,2048]{1,0:T(8,128)(2,1)}, u32[]{:S(2)}, u32[]{:S(2)}) collective-permute-start(bf16[112,2048]{1,0:T(8,128)(2,1)} %bitcast.29), channel_id=1, source_target_pairs={{0,80},{16,64},{64,16},{80,0},{1,81},{17,65},{65,17},{81,1},{2,82}... | collective-permute-start | bytes 1376264 | tf_op jit(solution)/shard_map/ppermute | solution.py:146
  69.4 1.3 %copy-start.2 = (bf16[1024,576]{1,0:T(8,128)(2,1)S(1)}, bf16[1024,576]{1,0:T(8,128)(2,1)}, u32[]{:S(2)}) copy-start(bf16[1024,576]{1,0:T(8,128)(2,1)} %reshape.38.key_ref) | copy-start | bytes 3538948
  82.7 13.5 %all-to-all-start.2 = ((bf16[8,24,1024]{2,1,0:T(8,128)(2,1)}), bf16[8,24,1024]{2,1,0:T(8,128)(2,1)S(1)}, u32[]{:S(2)}, u32[]{:S(2)}) async-start(bf16[8,24,1024]{2,1,0:T(8,128)(2,1)} %bitcast.14), calls=%async_computation.2 | async-start | bytes 786432 | tf_op jit(solution)/shard_map/all_to_all | solution.py:173
  86.2 8.4 %collective-permute-start.7 = (bf16[112,2048]{1,0:T(8,128)(2,1)}, bf16[112,2048]{1,0:T(8,128)(2,1)S(1)}, u32[]{:S(2)}, u32[]{:S(2)}) collective-permute-start(bf16[112,2048]{1,0:T(8,128)(2,1)} %collective-permute-done.4.refs_1_), channel_id=1, source_target_pairs={{0,8},{8,0},{1,9},{9,1},{2,10},{10,2},{3,11},{11,3},{4,12},{12,4},... | collective-permute-start | bytes 1376264 | tf_op jit(solution)/shard_map/ppermute | solution.py:26
  90.2 4.4 %collective-permute-start.8 = (bf16[112,2048]{1,0:T(8,128)(2,1)}, bf16[112,2048]{1,0:T(8,128)(2,1)S(1)}, u32[]{:S(2)}, u32[]{:S(2)}) collective-permute-start(bf16[112,2048]{1,0:T(8,128)(2,1)} %collective-permute-done.5.refs_2_), channel_id=1, source_target_pairs={{0,8},{8,0},{1,9},{9,1},{2,10},{10,2},{3,11},{11,3},{4,12},{12,4},... | collective-permute-start | bytes 1376264 | tf_op jit(solution)/shard_map/ppermute | solution.py:26
  92.1 4.0 %collective-permute-start.9 = (bf16[112,2048]{1,0:T(8,128)(2,1)}, bf16[112,2048]{1,0:T(8,128)(2,1)S(1)}, u32[]{:S(2)}, u32[]{:S(2)}) collective-permute-start(bf16[112,2048]{1,0:T(8,128)(2,1)} %collective-permute-done.6.refs_3_), channel_id=1, source_target_pairs={{0,8},{8,0},{1,9},{9,1},{2,10},{10,2},{3,11},{11,3},{4,12},{12,4},... | collective-permute-start | bytes 1376264 | tf_op jit(solution)/shard_map/ppermute | solution.py:26
  96.2 1.0 copy-start.3
